TPU v7x, 256 devices: a whole 4x4x8 slice. The times are simulated.
256 devices in a mesh: row: 8 (over z_hi, x), col: 32 (over y, z_lo, core).
Axes of the slice: x: 4, y: 4, z: 8 (z_hi: 2, z_lo: 4; z = z_hi * 4 + z_lo), core: 2. Of those that a mesh axis runs over, the one named last changes fastest.
Arguments:
- cotangent: bfloat16 [1024, 3584, 128], P('row', 'col'), may hold values from -6 to 6
- prev_pair: bfloat16 [1024, 3584, 128], P('row', 'col'), may hold values from -12 to 12
- single_rows: bfloat16 [1024, 384], P('row'), may hold values from -6 to 6
- single_cols: bfloat16 [3584, 384], P('col'), may hold values from -6 to 6
- w_row: bfloat16 [384, 128], replicated, may hold values from -0.3125 to 0.3125
- w_col: bfloat16 [384, 128], replicated, may hold values from -0.3125 to 0.3125
- w_rec: bfloat16 [128, 128], replicated, may hold values from -0.5 to 0.5
- ln_gain: float32 [128], replicated, may hold values from 0.25 to 1.75
- ln_bias: float32 [128], replicated, may hold values from -1 to 1
- ids_rows: int32 [5, 1024], P(None, 'row'), may hold values from 0 to 1087, as said below
- ids_cols: int32 [5, 3584], P(None, 'col'), may hold values from 0 to 3647, as said below
Outputs:
- d_prev: bfloat16 [1024, 3584, 128], P('row', 'col')
- d_single_rows: float32 [1024, 384], P('row')
- d_single_cols: float32 [3584, 384], P('col')
- d_w_row: float32 [384, 128], replicated
- d_w_col: float32 [384, 128], replicated
- d_w_rec: float32 [128, 128], replicated
- d_w_rel: float32 [139, 128], replicated
- d_gain: float32 [128], replicated
- d_bias: float32 [128], replicated
Inputs may be any that keep to these rules, and one draw needn't show every extreme that they name: `ids_rows`: ids rows in order: residue index, token index within its chain, chain id, entity id, symmetry id (the number of earlier chains of the same entity). Chains are contiguous; in ligand chains all tokens share one residue index; the first chain is a ligand of at least 48 tokens. The band's rows are the first 1024 column tokens, with the same ids. `ids_cols`: same layout as ids_rows; where there are more column tokens than rows, a chain begins at column token 1024.
All inputs are finite; a program needn't handle non-finite values.
Results may differ from a plain program's by a relative error of at most 0.003.
Values sent between devices are 32-bit elements; how exact they have to be, the bound alone decides.
No kernel may reach another device: no remote copies, remote signals or barrier semaphores. Data moves between devices by JAX's collectives and lax.ppermute only.
A program may use at most 64 MiB of HBM per device.

v0:
```python
import jax
import jax.numpy as jnp
from jax import lax
from jax.sharding import PartitionSpec as P


def layer_terms(cot, prev, norm_gain, norm_bias, w_rec):
    width = cot.shape[-1]
    flat_cot = cot.reshape(-1, width)
    x = prev.reshape(-1, width).astype(jnp.float32)
    input_mean = jnp.mean(x, axis=1, keepdims=True)
    centered_input = x - input_mean
    inverse_deviation = lax.rsqrt(
        jnp.mean(centered_input * centered_input, axis=1, keepdims=True) + 1e-05
    )
    standardized_input = centered_input * inverse_deviation
    normalized_input = (standardized_input * norm_gain + norm_bias).astype(jnp.bfloat16)
    rec_grad = lax.dot_general(
        normalized_input, flat_cot, (((0,), (0,)), ((), ())), preferred_element_type=jnp.float32
    )
    output_gradient = lax.dot_general(
        flat_cot, w_rec, (((1,), (1,)), ((), ())), preferred_element_type=jnp.float32
    )
    norm_gain_gradient = jnp.sum(output_gradient * standardized_input, axis=0)
    bias_grad = jnp.sum(output_gradient, axis=0)
    scaled_gradient = output_gradient * norm_gain
    backward_result = inverse_deviation * (
        scaled_gradient
        - jnp.mean(scaled_gradient, axis=1, keepdims=True)
        - standardized_input * jnp.mean(scaled_gradient * standardized_input, axis=1, keepdims=True)
    )
    return (
        backward_result.astype(jnp.bfloat16).reshape(cot.shape),
        rec_grad,
        norm_gain_gradient,
        bias_grad,
    )


def bin_table(index, count, flat_cot):
    onehot = (jnp.arange(count, dtype=jnp.int32)[:, None] == index[None, :]).astype(jnp.bfloat16)
    return jnp.dot(onehot, flat_cot, preferred_element_type=jnp.float32)


def relpos_grad(ids_i, ids_j, flat_cot):
    same_chain = ids_i[2][:, None] == ids_j[2][None, :]
    same_res = same_chain & (ids_i[0][:, None] == ids_j[0][None, :])
    same_entity = ids_i[3][:, None] == ids_j[3][None, :]
    res_bin = jnp.where(
        same_chain, jnp.clip(ids_i[0][:, None] - ids_j[0][None, :] + 32, 0, 64), 65
    ).reshape(-1)
    tok_bin = jnp.where(
        same_res, jnp.clip(ids_i[1][:, None] - ids_j[1][None, :] + 32, 0, 64), 65
    ).reshape(-1)
    chain_bin = jnp.where(
        same_entity & jnp.logical_not(same_chain),
        jnp.clip(ids_i[4][:, None] - ids_j[4][None, :] + 2, 0, 4),
        5,
    ).reshape(-1)
    entity_row = same_entity.reshape(1, -1).astype(jnp.bfloat16)
    parts = [
        bin_table(res_bin, 66, flat_cot),
        bin_table(tok_bin, 66, flat_cot),
        jnp.dot(entity_row, flat_cot, preferred_element_type=jnp.float32),
        bin_table(chain_bin, 6, flat_cot),
    ]
    return jnp.concatenate(parts, axis=0)


def shards(
    cotangent,
    prev_pair,
    single_rows,
    single_cols,
    w_row,
    w_col,
    w_rec,
    ln_gain,
    ln_bias,
    ids_rows,
    ids_cols,
):
    width = cotangent.shape[-1]
    high = lax.Precision.HIGHEST
    backward_result, rec_grad, norm_gain_gradient, bias_grad = layer_terms(
        cotangent, prev_pair, ln_gain, ln_bias, w_rec
    )
    rel_grad = relpos_grad(ids_rows, ids_cols, cotangent.reshape(-1, width))
    row_part = jnp.sum(cotangent, axis=1, dtype=jnp.float32)
    col_part = jnp.sum(cotangent, axis=0, dtype=jnp.float32)
    row_proj = w_row.astype(jnp.float32)
    col_proj = w_col.astype(jnp.float32)
    row_sum = lax.psum(row_part, "col")
    col_sum = lax.psum(col_part, "row")
    d_single_rows = jnp.dot(row_sum, row_proj.T, precision=high)
    d_single_cols = jnp.dot(col_sum, col_proj.T, precision=high)
    row_weight = jnp.dot(single_rows.astype(jnp.float32).T, row_sum, precision=high)
    col_weight = jnp.dot(single_cols.astype(jnp.float32).T, col_sum, precision=high)
    d_w_row = lax.psum(row_weight, "row")
    d_w_col = lax.psum(col_weight, "col")
    rec_grad, rel_grad, norm_gain_gradient, bias_grad = lax.psum(
        (rec_grad, rel_grad, norm_gain_gradient, bias_grad), ("row", "col")
    )
    return (
        backward_result,
        d_single_rows,
        d_single_cols,
        d_w_row,
        d_w_col,
        rec_grad,
        rel_grad,
        norm_gain_gradient,
        bias_grad,
    )


def solution(mesh):
    return jax.shard_map(
        shards,
        mesh=mesh,
        in_specs=(
            P("row", "col", None),
            P("row", "col", None),
            P("row", None),
            P("col", None),
            P(),
            P(),
            P(),
            P(),
            P(),
            P(None, "row"),
            P(None, "col"),
        ),
        out_specs=(
            P("row", "col", None),
            P("row", None),
            P("col", None),
            P(),
            P(),
            P(),
            P(),
            P(),
            P(),
        ),
        check_vma=False,
    )
```

profile of v0, /device:TPU:1, one launch (start us, length us, event | category | flops | bytes accessed | tf_op | source)
XLA Modules:
  0.0 703.4 jit_solution(13627841183170476321)
XLA Ops:
  7.2 0.0 copy-start
  7.2 0.0 all-reduce.11.cloned.1.call-start
  7.3 5.5 convert_reduce_fusion
  12.8 49.6 %psum.57 = f32[112,128]{1,0:T(8,128)S(1)} all-reduce(f32[112,128]{1,0:T(8,128)S(1)} %get-tuple-element.33), channel_id=1, replica_groups=mesh['row'=8,'col'=32] {'row'}, use_global_device_ids=true, to_apply=%region_7.8 | all-reduce | flops 14336 | bytes 114688 | tf_op jit(solution)/shard_map/psum | solution.py:94
  62.4 1.9 convolution_bitcast_fusion
  64.2 0.0 all-reduce.11.cloned.1.call-update
  64.2 0.0 copy-start.9
  64.3 0.0 copy-start.12
  64.3 0.0 all-reduce.7.cloned.1.call-start
  64.3 3.2 convert_reduce_fusion.2
  67.6 5.7 multiply_reduce_fusion.2
  73.4 0.2 compare_select_fusion
  73.5 0.1 select_n.26
  73.7 0.1 reshape.243
  73.8 2.9 fusion.1
  76.6 2.9 fusion.2
  79.5 0.1 reshape.246
  79.6 0.0 copy-done.9
  79.6 0.0 copy-done.12
  79.6 0.0 copy-start.1
  79.7 8.4 %fusion.10 = f32[128,128]{1,0:T(8,128)} fusion(bf16[128,112,128]{2,1,0:T(8,128)(2,1)} %param.11, bf16[128,112,128]{2,1,0:T(8,128)(2,1)} %param.12, f32[128]{0:T(128)S(1)} %copy-done.12, f32[128]{0:T(128)S(1)} %copy-done.9, f32[128,112]{1,0:T(8,128)S(1)} %add_rsqrt_fusion, f32[128,112]{1,0:T(8,128)S(1)} %broadcast_multiply_fusion), kind=kOutput, calls=%fused_computation.24 | convolution fusion | flops 480772096 | bytes 7521280 | tf_op jit(solution)/shard_map/dot_general | solution.py:18
  88.1 0.6 fusion.11
  88.7 0.1 compare_bitcast_fusion
  88.8 252.5 %all-reduce.11.cloned.1.call-done = (f32[128,128]{1,0:T(8,128)}, f32[384,128]{0,1:T(8,128)}) async-done(((f32[128,128]{1,0:T(8,128)}, f32[384,128]{0,1:T(8,128)}), (f32[128,128]{1,0:T(8,128)}, f32[384,128]{0,1:T(8,128)})) %all-reduce.11.cloned.1.call-update) | async-done | bytes 262160 | tf_op jit(solution)/shard_map/psum | solution.py:93
  341.2 1.8 convolution_bitcast_fusion.1
  343.0 0.0 all-reduce.7.cloned.1.call-update
  343.0 0.0 copy-start.8
  343.1 0.2 all-reduce.9.cloned.1.call-start
  343.3 3.2 convolution_bitcast_fusion.2
  346.5 0.7 pad_maximum_fusion
  347.1 0.0 all-reduce.9.cloned.1.call-update
  347.2 0.1 rsqrt.13
  347.3 0.1 div.17
  347.4 0.0 copy-done.6
  347.4 0.0 copy-start.2
  347.4 0.0 copy-start.3
  347.4 0.9 fusion.16
  348.3 9.3 %fusion = f32[14336,128]{1,0:T(8,128)S(1)} fusion(bf16[128,112,128]{2,1,0:T(8,128)(2,1)} %param.12, f32[14336]{0:T(1024)S(1)} %div.17, f32[14336]{0:T(1024)S(1)} %rsqrt.13), kind=kLoop, calls=%fused_computation.3 | loop fusion | flops 5505024 | bytes 11124736 | tf_op jit(solution)/shard_map/mul | solution.py:16
  357.7 12.4 %fusion.14 = (f32[128]{0:T(128)S(1)}, f32[128]{0:T(128)S(1)}, f32[14336]{0:T(1024)S(1)}, f32[14336]{0:T(1024)S(1)}, f32[14336,128]{1,0:T(8,128)}) fusion(f32[14336]{0:T(1024)S(1)} %rsqrt.13, f32[14336]{0:T(1024)S(1)} %div.17, bf16[128,112,128]{2,1,0:T(8,128)(2,1)S(1)} %copy-done.3, f32[14336,128]{1,0:T(8,128)S(1)} %fusion, f32[128]{0:T(128)S(1)} %copy-done.9, ...), kind=kOutput, calls=%fused_computation.52 | convolution fusion | flops 488083200 | bytes 22283776 | tf_op jit(solution)/shard_map/dot_general | solution.py:21
  370.1 78.7 %all-reduce = (f32[128]{0:T(128)}, f32[128]{0:T(128)}) all-reduce(f32[128]{0:T(128)S(1)} %get-tuple-element.30, f32[128]{0:T(128)S(1)} %get-tuple-element.29), channel_id=1, replica_groups=mesh['row'=8,'col'=32] {'row','col'}, use_global_device_ids=true, to_apply=%region_13.14 | all-reduce | flops 256 | bytes 2048 | tf_op jit(solution)/shard_map/psum | solution.py:101
  448.9 12.7 %multiply_convert_fusion = bf16[14336,128]{1,0:T(8,128)(2,1)} fusion(f32[14336,128]{1,0:T(8,128)} %get-tuple-element.54, f32[14336]{0:T(1024)S(1)} %get-tuple-element.55, f32[14336]{0:T(1024)S(1)} %get-tuple-element.56, f32[128]{0:T(128)S(1)} %copy-done.9, f32[14336]{0:T(1024)S(1)} %rsqrt.13, f32[14336]{0:T(1024)S(1)} %div.17, bf16[128,112,128]{2,1,0:T(8,128)(2,1)} %param.12), kind=kLoop, calls=%fused_computation.6 | loop fusion | flops 16515072 | bytes 14909952 | tf_op jit(solution)/shard_map/convert_element_type | solution.py:33
  461.6 0.0 copy-done.4
  461.6 0.9 fusion.15
  462.5 0.8 copy.27
  463.3 1.7 copy.26
  465.1 228.8 %all-reduce.9.cloned.1.call-done = (f32[128,128]{1,0:T(8,128)}, f32[139,128]{1,0:T(8,128)}) async-done(((f32[128,128]{1,0:T(8,128)}, f32[139,128]{1,0:T(8,128)}), (f32[128,128]{1,0:T(8,128)}, f32[139,128]{1,0:T(8,128)})) %all-reduce.9.cloned.1.call-update) | async-done | bytes 136720 | tf_op jit(solution)/shard_map/psum | solution.py:101
  693.9 1.5 copy.39
  695.4 1.5 copy.40
  (21 shorter events, 0.1 us)
Async XLA Ops:
  7.2 334.0 %copy-start = (bf16[128,384]{1,0:T(8,128)(2,1)S(1)}, bf16[128,384]{1,0:T(8,128)(2,1)}, u32[]{:S(2)}) copy-start(bf16[128,384]{1,0:T(8,128)(2,1)} %param.13) | copy-start | bytes 294916
  7.2 66.1 %copy-start.10 = (s32[5,128]{1,0:T(8,128)S(1)}, s32[5,128]{1,0:T(8,128)}, u32[]{:S(2)}) copy-start(s32[5,128]{1,0:T(8,128)} %param.20) | copy-start | bytes 7684
  7.2 66.2 %copy-start.11 = (s32[5,112]{1,0:T(8,128)S(1)}, s32[5,112]{1,0:T(8,128)}, u32[]{:S(2)}) copy-start(s32[5,112]{1,0:T(8,128)} %param.21) | copy-start | bytes 6724
  7.2 334.0 %all-reduce.11.cloned.1.call-start = ((), (), s32[]{:S(2)}) async-start(), calls=%async_computation.2 | async-start | bytes 524288 | tf_op jit(solution)/shard_map/psum | solution.py:93
  64.2 15.4 %copy-start.9 = (f32[128]{0:T(128)S(1)}, f32[128]{0:T(128)}, u32[]{:S(2)}) copy-start(f32[128]{0:T(128)} %param.18) | copy-start | bytes 1540
  64.3 15.4 %copy-start.12 = (f32[128]{0:T(128)S(1)}, f32[128]{0:T(128)}, u32[]{:S(2)}) copy-start(f32[128]{0:T(128)} %param.19) | copy-start | bytes 1540
  64.3 399.1 %all-reduce.7.cloned.1.call-start = ((), (), s32[]{:S(2)}) async-start(), calls=%async_computation | async-start | bytes 393216 | tf_op jit(solution)/shard_map/psum | solution.py:99
  79.6 8.4 %copy-start.1 = (bf16[128,112,128]{2,1,0:T(8,128)(2,1)S(1)}, bf16[128,112,128]{2,1,0:T(8,128)(2,1)}, u32[]{:S(2)}) copy-start(bf16[128,112,128]{2,1,0:T(8,128)(2,1)} %param.11) | copy-start | bytes 11010052
  88.1 259.3 %copy-start.6 = (bf16[384,128]{1,0:T(8,128)(2,1)S(1)}, bf16[384,128]{1,0:T(8,128)(2,1)}, u32[]{:S(2)}) copy-start(bf16[384,128]{1,0:T(8,128)(2,1)} %param.16) | copy-start | bytes 294916
  343.0 14.6 %copy-start.8 = (bf16[128,128]{1,0:T(8,128)(2,1)S(1)}, bf16[128,128]{1,0:T(8,128)(2,1)}, u32[]{:S(2)}) copy-start(bf16[128,128]{1,0:T(8,128)(2,1)} %param.17) | copy-start | bytes 98308
  343.1 350.8 %all-reduce.9.cloned.1.call-start = ((), (), s32[]{:S(2)}) async-start(), calls=%async_computation.1 | async-start | bytes 278528 | tf_op jit(solution)/shard_map/psum | solution.py:101
  347.4 10.3 %copy-start.2 = (bf16[128,112,128]{2,1,0:T(8,128)(2,1)S(1)}, bf16[128,112,128]{2,1,0:T(8,128)(2,1)}, u32[]{:S(2)}) copy-start(bf16[128,112,128]{2,1,0:T(8,128)(2,1)} %param.11) | copy-start | bytes 11010052
  347.4 10.3 %copy-start.3 = (bf16[128,112,128]{2,1,0:T(8,128)(2,1)S(1)}, bf16[128,112,128]{2,1,0:T(8,128)(2,1)}, u32[]{:S(2)}) copy-start(bf16[128,112,128]{2,1,0:T(8,128)(2,1)} %param.12) | copy-start | bytes 11010052
  448.9 12.7 %copy-start.4 = (f32[128,128]{1,0:T(8,128)S(1)}, f32[128,128]{1,0:T(8,128)}, u32[]{:S(2)}) copy-start(f32[128,128]{1,0:T(8,128)} %get-tuple-element.39) | copy-start | bytes 196612
  448.9 12.7 %copy-start.7 = (bf16[384,128]{1,0:T(8,128)(2,1)S(1)}, bf16[384,128]{1,0:T(8,128)(2,1)}, u32[]{:S(2)}) copy-start(bf16[384,128]{1,0:T(8,128)(2,1)} %param.15) | copy-start | bytes 294916
  448.9 13.7 %copy-start.5 = (f32[384,128]{0,1:T(8,128)S(1)}, f32[384,128]{0,1:T(8,128)}, u32[]{:S(2)}) copy-start(f32[384,128]{0,1:T(8,128)} %get-tuple-element.40) | copy-start | bytes 589828
Sparse Core Ops, SparseCore 0:
  64.4 276.8 all-reduce.10
  344.6 99.6 all-reduce.6
  450.5 243.3 all-reduce.8
where the time goes:
time: 704 us; the launch traced here: 703 us
  waiting for transfers between devices  481 us (68%)
  blocking collectives  128 us (18%)
  other arithmetic  37.4 us (5%)
  matrix products  35.9 us (5%)
  between operations  14 us (2%)
    psum x1, waiting for transfers between devices, shards(): row_sum = lax.psum(row_part, 'col')  252 us
    psum x1, waiting for transfers between devices, shards(): lax.psum((rec_grad, rel_grad, norm_gain_gradient, bias_grad), ('row', 'co...  229 us
    psum x1, blocking collectives, shards(): lax.psum((rec_grad, rel_grad, norm_gain_gradient, bias_grad), ('row', 'co...  78.7 us
    psum x1, blocking collectives, shards(): col_sum = lax.psum(col_part, 'row')  49.6 us
  transfers between devices with their start and end apart: 3, of which 2 were waited for; matrix products, arithmetic and copies ran while one was open for 10% of the time, Pallas kernels for 0%

commit v1 on v0

v1 whole, which is shorter than its diff:
```python
import functools

import jax
import jax.numpy as jnp
from jax import lax
from jax.experimental import pallas as pl
from jax.experimental.pallas import tpu as pltpu
from jax.sharding import Mesh, PartitionSpec as P

F32, BF16 = jnp.float32, jnp.bfloat16
C = 128
S = 384
BINS = 139
SUB = 8
CHUNK = 40
PARTS = 32
ROW = ("zh", "x")
COLG = ("y", "zl")


def dot(a, b, dims):
    return lax.dot_general(a, b, (dims, ((), ())), preferred_element_type=F32)


def split_dot(a, b, dims, split_left):
    x = a if split_left else b
    hi = x.astype(BF16)
    rest = x - hi.astype(F32)
    mid = rest.astype(BF16)
    low = (rest - mid.astype(F32)).astype(BF16)
    if split_left:
        return dot(hi, b, dims) + (dot(mid, b, dims) + dot(low, b, dims))
    return dot(a, hi, dims) + (dot(a, mid, dims) + dot(a, low, dims))


def standardize(prev):
    ones = jnp.full((C, C), 1.0 / C, BF16)
    mean = dot(prev, ones, ((1,), (0,)))
    centered = prev.astype(F32) - mean
    var = dot((centered * centered).astype(BF16), ones, ((1,), (0,)))
    rstd = lax.rsqrt(var + 1e-05)
    return centered * rstd, rstd


def reduce_kernel(cols, steps, rows, core_ref, cot_ref, prev_ref, idr_ref, idc_ref, sr_ref, sc_ref,
                  send_ref, keep_ref, colp_ref, acc, rowp, colp, buf):
    step = pl.program_id(0)

    @pl.when(step == 0)
    def _():
        acc[...] = jnp.zeros_like(acc)
        colp[...] = jnp.zeros_like(colp)

    n = SUB * cols
    idr = idr_ref[...].astype(F32)
    idc = idc_ref[...].astype(F32)
    lane = lax.broadcasted_iota(jnp.int32, (SUB, idr.shape[1]), 1)
    sub = lax.broadcasted_iota(jnp.int32, (SUB, idr.shape[1]), 0)
    flat_lane = lax.broadcasted_iota(jnp.int32, (16, n), 1)
    flat_sub = lax.broadcasted_iota(jnp.int32, (16, n), 0)
    rowind = jnp.where((flat_lane >= flat_sub * cols) & (flat_lane < (flat_sub + 1) * cols), 1.0, 0.0).astype(BF16)

    for b in range(rows // SUB):
        first = step * rows + b * SUB
        cot = cot_ref[b * SUB:(b + 1) * SUB].reshape(n, C)
        prev = prev_ref[b * SUB:(b + 1) * SUB].reshape(n, C)
        xhat, _ = standardize(prev)
        mask = lane == sub + first
        di = [jnp.sum(jnp.where(mask, idr[k:k + 1], 0.0), axis=1, keepdims=True) for k in range(5)]
        dj = [idc[k:k + 1] for k in range(5)]
        same_chain = di[2] == dj[2]
        same_res = same_chain & (di[0] == dj[0])
        same_entity = di[3] == dj[3]
        r = jnp.where(same_chain, jnp.clip(di[0] - dj[0] + 32.0, 0.0, 64.0), 65.0)
        t = jnp.where(same_res, jnp.clip(di[1] - dj[1] + 32.0, 0.0, 64.0), 65.0) + 66.0
        e = jnp.where(same_entity, 132.0, -1.0)
        c = jnp.where(same_entity & jnp.logical_not(same_chain), jnp.clip(di[4] - dj[4] + 2.0, 0.0, 4.0), 5.0) + 133.0
        r, t, e, c = [
            jnp.concatenate([v[s:s + 1] for s in range(SUB)], axis=1) for v in (r, t, e, c)
        ]

        def hot(lo, hi, *codes):
            q = lax.broadcasted_iota(jnp.int32, (hi - lo, n), 0).astype(F32) + float(lo)
            hit = q == codes[0]
            for code in codes[1:]:
                hit = hit | (q == code)
            return jnp.where(hit, 1.0, 0.0).astype(BF16)

        left = jnp.concatenate(
            [
                jnp.transpose(xhat.astype(BF16)),
                hot(0, 64, r), hot(64, 80, r, t), hot(80, 128, t), hot(128, 144, t, e, c),
                rowind,
            ],
            axis=0,
        )
        out = dot(left, cot, ((1,), (0,)))
        acc[...] += out[:272]
        rowp[pl.ds(pl.multiple_of(first, SUB), SUB), :] = out[272:280]
        wide = cot_ref[b * SUB].astype(F32)
        for s in range(1, SUB):
            wide += cot_ref[b * SUB + s].astype(F32)
        colp[...] += wide

    @pl.when(step == steps - 1)
    def _():
        dwr = split_dot(sr_ref[...], rowp[...], ((0,), (0,)), False)
        dwc = split_dot(sc_ref[...], colp[...], ((0,), (0,)), False)
        total = acc[...]
        colp_ref[...] = colp[...]
        for k in range(PARTS):
            half, place = k // 16, k % 16
            buf[half, place, 0:4] = total[4 * k:4 * k + 4]
            buf[half, place, 4:8] = rowp[4 * k:4 * k + 4]
            lo, hi = 128 + 5 * k, min(128 + 5 * k + 5, 272)
            if lo < hi:
                buf[half, place, 8:8 + hi - lo] = total[lo:hi]
            pad = 8 + max(hi - lo, 0)
            buf[half, place, pad:16] = jnp.zeros((16 - pad, C), F32)
            buf[half, place, 16:28] = dwr[12 * k:12 * k + 12]
            buf[half, place, 28:40] = dwc[12 * k:12 * k + 12]
        core = core_ref[0]
        keep_ref[...] = buf[core]
        send_ref[...] = buf[1 - core]


def local_reductions(core, cot, prev, idr, idc, sr, sc):
    rows, cols = cot.shape[:2]
    per = 16
    steps = rows // per
    whole = lambda a: pl.BlockSpec(a.shape, lambda i: (0,) * a.ndim)
    part = jax.ShapeDtypeStruct((16, CHUNK, C), F32)
    colo = jax.ShapeDtypeStruct((cols, C), F32)
    return pl.pallas_call(
        functools.partial(reduce_kernel, cols, steps, per),
        grid=(steps,),
        in_specs=[
            pl.BlockSpec(memory_space=pltpu.SMEM),
            pl.BlockSpec((per, cols, C), lambda i: (i, 0, 0)),
            pl.BlockSpec((per, cols, C), lambda i: (i, 0, 0)),
            whole(idr), whole(idc), whole(sr), whole(sc),
        ],
        out_specs=[whole(part), whole(part), whole(colo)],
        out_shape=[part, part, colo],
        scratch_shapes=[
            pltpu.VMEM((272, C), F32),
            pltpu.VMEM((rows, C), F32),
            pltpu.VMEM((cols, C), F32),
            pltpu.VMEM((2, 16, CHUNK, C), F32),
        ],
        compiler_params=pltpu.CompilerParams(vmem_limit_bytes=48 * 1024 * 1024),
        name="local_reductions",
    )(core, cot, prev, idr, idc, sr, sc)


def prev_kernel(cols, rows, cot_ref, prev_ref, w_ref, gain_ref, *rest):
    out_ref = rest[-1]
    n = SUB * cols
    gain = gain_ref[...]
    w = w_ref[...]
    gain_mean = jnp.sum(w.astype(F32) * jnp.transpose(jnp.broadcast_to(gain, (C, C))), axis=0, keepdims=True) * (1.0 / C)
    mean_w = jnp.broadcast_to(gain_mean, (C, C)).astype(BF16)
    both = jnp.concatenate([w, mean_w], axis=0)
    ones = jnp.full((C, C), 1.0 / C, BF16)
    for b in range(rows // SUB):
        cot = cot_ref[b * SUB:(b + 1) * SUB].reshape(n, C)
        prev = prev_ref[b * SUB:(b + 1) * SUB].reshape(n, C)
        xhat, rstd = standardize(prev)
        y = dot(cot, both, ((1,), (1,)))
        g = y[:, :C] * gain
        corr = dot((g * xhat).astype(BF16), ones, ((1,), (0,)))
        res = rstd * (g - y[:, C:] - xhat * corr)
        out_ref[b * SUB:(b + 1) * SUB] = res.astype(BF16).reshape(SUB, cols, C)


def prev_grad(lo, hi, per, cot, prev, w, gain, into):
    rows, cols = cot.shape[:2]
    block = pl.BlockSpec((per, cols, C), lambda i: (lo // per + i, 0, 0))
    args = [cot, prev, w, gain]
    specs = [block, block, pl.BlockSpec((C, C), lambda i: (0, 0)), pl.BlockSpec((1, C), lambda i: (0, 0))]
    if into is not None:
        args.append(into)
        specs.append(pl.BlockSpec(memory_space=pl.ANY))
    pairs = (hi - lo) * cols
    return pl.pallas_call(
        functools.partial(prev_kernel, cols, per),
        grid=((hi - lo) // per,),
        in_specs=specs,
        out_specs=block,
        out_shape=jax.ShapeDtypeStruct(cot.shape, BF16),
        input_output_aliases={4: 0} if into is not None else {},
        compiler_params=pltpu.CompilerParams(vmem_limit_bytes=48 * 1024 * 1024),
        cost_estimate=pl.CostEstimate(flops=pairs * C * C * 10, bytes_accessed=pairs * C * 6, transcendentals=0),
        name="prev_grad",
    )(*args)


def final_kernel(core_ref, own_ref, other_ref, cols_ref, wr_ref, wc_ref, w_ref, gain_ref, bias_ref,
                 dsr_ref, dsc_ref, dwr_ref, dwc_ref, rec_ref, rel_ref, dg_ref, db_ref, buf, m, rows, rel):
    core = core_ref[0]
    buf[core] = own_ref[...]
    buf[1 - core] = other_ref[...]
    for k in range(PARTS):
        half, place = k // 16, k % 16
        m[4 * k:4 * k + 4] = buf[half, place, 0:4]
        rows[4 * k:4 * k + 4] = buf[half, place, 4:8]
        lo, hi = 5 * k, min(5 * k + 5, 144)
        if lo < hi:
            rel[lo:hi] = buf[half, place, 8:8 + hi - lo]
        dwr_ref[12 * k:12 * k + 12] = buf[half, place, 16:28]
        dwc_ref[12 * k:12 * k + 12] = buf[half, place, 28:40]
    rel_ref[...] = rel[0:BINS]
    total = jnp.sum(rel[133:139], axis=0, keepdims=True)
    big = m[...]
    w = w_ref[...].astype(F32)
    gain_col = jnp.transpose(jnp.broadcast_to(gain_ref[...], (C, C)))
    bias_col = jnp.transpose(jnp.broadcast_to(bias_ref[...], (C, C)))
    rec_ref[...] = gain_col * big + bias_col * total
    dg_ref[...] = jnp.sum(jnp.transpose(w * big), axis=0, keepdims=True)
    db_ref[...] = jnp.sum(jnp.transpose(w * total), axis=0, keepdims=True)
    dsr_ref[...] = split_dot(rows[...], wr_ref[...], ((1,), (1,)), True)
    dsc_ref[...] = split_dot(cols_ref[...], wc_ref[...], ((1,), (1,)), True)


def finish(core, own, other, cols, wr, wc, w, gain, bias, nrows):
    f = lambda *s: jax.ShapeDtypeStruct(s, F32)
    vmem = pl.BlockSpec(memory_space=pltpu.VMEM)
    return pl.pallas_call(
        final_kernel,
        in_specs=[pl.BlockSpec(memory_space=pltpu.SMEM)] + [vmem] * 8,
        out_specs=[vmem] * 8,
        out_shape=[f(nrows, S), f(cols.shape[0], S), f(S, C), f(S, C), f(C, C), f(BINS, C), f(1, C), f(1, C)],
        scratch_shapes=[
            pltpu.VMEM((2, 16, CHUNK, C), F32),
            pltpu.VMEM((C, C), F32),
            pltpu.VMEM((nrows, C), F32),
            pltpu.VMEM((144, C), F32),
        ],
        compiler_params=pltpu.CompilerParams(vmem_limit_bytes=48 * 1024 * 1024),
        name="finish",
    )(core, own, other, cols, wr, wc, w, gain, bias)


def swap(a, axis, size, bit):
    return lax.ppermute(a, axis, [(i, i ^ bit) for i in range(size)])


def shards(cot, prev, single_rows, single_cols, w_row, w_col, w_rec, gain, bias, ids_rows, ids_cols):
    core = lax.axis_index("c").astype(jnp.int32).reshape(1)
    gain2, bias2 = gain.reshape(1, C), bias.reshape(1, C)
    send, keep, col_part = local_reductions(core, cot, prev, ids_rows, ids_cols, single_rows, single_cols)
    half = keep + swap(send, "c", 2, 1)
    chunks = lax.all_to_all(half, COLG, 0, 0)
    mine = jnp.sum(chunks, axis=0)
    z = jnp.concatenate([mine, col_part], axis=0)
    d_prev = None
    cuts = (0, 32, 80, 128)
    for turn, (axis, size, bit) in enumerate((("x", 4, 1), ("x", 4, 3), ("zh", 2, 1))):
        got = swap(z, axis, size, bit)
        if d_prev is None:
            c2, p2, z = lax.optimization_barrier((cot, prev, z))
        else:
            d_prev, z = lax.optimization_barrier((d_prev, z))
        d_prev = prev_grad(cuts[turn], cuts[turn + 1], 16, c2, p2, w_rec, gain2, d_prev)
        z = z + got
    kept = lax.broadcasted_iota(jnp.int32, (CHUNK, 1), 0) // 4 == 1
    full = jnp.where(kept, mine, z[:CHUNK])
    col_sum = z[CHUNK:]
    own = lax.all_to_all(jnp.broadcast_to(full[None], (16, CHUNK, C)), COLG, 0, 0)
    other = swap(own, "c", 2, 1)
    dsr, dsc, dwr, dwc, rec, rel, dg, db = finish(
        core, own, other, col_sum, w_row, w_col, w_rec, gain2, bias2, cot.shape[0]
    )
    return d_prev, dsr, dsc, dwr, dwc, rec, rel, dg.reshape(C), db.reshape(C)


def solution(mesh):
    fine = Mesh(mesh.devices.reshape(2, 4, 4, 4, 2), ("zh", "x", "y", "zl", "c"))
    row, col = ROW, COLG + ("c",)
    return jax.shard_map(
        shards,
        mesh=fine,
        in_specs=(
            P(row, col, None), P(row, col, None), P(row, None), P(col, None),
            P(), P(), P(), P(), P(), P(None, row), P(None, col),
        ),
        out_specs=(P(row, col, None), P(row, None), P(col, None), P(), P(), P(), P(), P(), P()),
        check_vma=False,
    )
```

time: 704 us -> 84.9 us (0.12)
  waiting for transfers between devices: 481 us -> 3.3 us
  blocking collectives: 128 us -> 30.2 us
  other arithmetic: 37.4 us -> 0.18 us
  matrix products: 35.9 us -> 0 us
  Pallas kernels: 0 us -> 26.8 us
  starting transfers between devices: 0.3 us -> 15.9 us
  between operations: 14 us -> 0.75 us
    psum x3 -> x0, waiting for transfers between devices: 481 us -> none  [the longest x1 252 us: shards(): row_sum = lax.psum(row_part, 'col')]
    psum x2 -> x0, blocking collectives: 128 us -> none  [the longest x1 78.7 us: shards(): lax.psum((rec_grad, rel_grad, norm_gain_gradient, bias_grad), ('row', 'co...]
    dot_general x10 -> x0, matrix products: 35.9 us -> none  [the longest x1 12.4 us: layer_terms(): lax.dot_general(flat_cot, w_rec, (((1,), (1,)), ((), ())), preferred_elem...]
    all_to_all x0 -> x2, blocking collectives: none -> 30.2 us  [the longest x1 17.7 us: shards(): chunks = lax.all_to_all(half, COLG, 0, 0)]
    pallas_call x0 -> x5, Pallas kernels: none -> 26.8 us  [the longest x3 14.4 us: prev_grad(): pl.pallas_call(functools.partial(prev_kernel, cols, per), grid=((hi - lo)...]
    ppermute x0 -> x5, starting transfers between devices: none -> 15.9 us  [swap(): return lax.ppermute(a, axis, [(i, i ^ bit) for i in range(size)])]
    reduce_sum x3 -> x1, other arithmetic: 14.5 us -> 0.02 us  [shards(): mine = jnp.sum(chunks, axis=0)]
    convert_element_type x1 -> x0, other arithmetic: 12.7 us -> none  [layer_terms(): backward_result.astype(jnp.bfloat16).reshape(cot.shape)]
  transfers between devices with their start and end apart: 3 -> 5, of which waited for: 2 -> 2; matrix products, arithmetic and copies ran while one was open for 10% -> 0% of each run, Pallas kernels for 0% -> 17%
where the time goes in v1:
time: 84.9 us; the launch traced here: 84.4 us
  blocking collectives  30.2 us (36%)
  Pallas kernels  26.8 us (32%)
  starting transfers between devices  15.9 us (19%)
  local copies, waits for them, and re-layouts  7.27 us (9%)
  waiting for transfers between devices  3.3 us (4%)
    all_to_all x1, blocking collectives, shards(): chunks = lax.all_to_all(half, COLG, 0, 0)  17.7 us
    ppermute x5, starting transfers between devices, swap(): return lax.ppermute(a, axis, [(i, i ^ bit) for i in range(size)])  15.9 us
    pallas_call x3, Pallas kernels, prev_grad(): pl.pallas_call(functools.partial(prev_kernel, cols, per), grid=((hi - lo)...  14.4 us
    all_to_all x1, blocking collectives, shards(): lax.all_to_all(jnp.broadcast_to(full[None], (16, CHUNK, C)), COLG, 0, 0)  12.5 us
    pallas_call x1, Pallas kernels, local_reductions(): pl.pallas_call(functools.partial(reduce_kernel, cols, steps, per), grid=(...  11.2 us
    unnamed x22, local copies, waits for them, and re-layouts  7.24 us
    ppermute x5, waiting for transfers between devices, swap(): return lax.ppermute(a, axis, [(i, i ^ bit) for i in range(size)])  3.3 us
  transfers between devices with their start and end apart: 5, of which 2 were waited for; matrix products, arithmetic and copies ran while one was open for 0% of the time, Pallas kernels for 17%

profile of v1, /device:TPU:1, one launch (start us, length us, event | category | flops | bytes accessed | tf_op | source)
XLA Modules:
  0.0 84.4 jit_solution(3608059306676851289)
XLA Ops:
  0.6 0.0 copy-start
  0.7 2.0 %copy-done = bf16[128,112,128]{2,1,0:T(8,128)(2,1)S(1)} copy-done((bf16[128,112,128]{2,1,0:T(8,128)(2,1)S(1)}, bf16[128,112,128]{2,1,0:T(8,128)(2,1)}, u32[]{:S(2)}) %copy-start) | copy-done | bytes 3670040
  2.7 0.0 copy-start.3
  2.7 0.9 %copy-done.3 = bf16[128,384]{1,0:T(8,128)(2,1)S(1)} copy-done((bf16[128,384]{1,0:T(8,128)(2,1)S(1)}, bf16[128,384]{1,0:T(8,128)(2,1)}, u32[]{:S(2)}) %copy-start.3) | copy-done | bytes 98328
  3.6 0.0 copy-start.6
  3.6 0.9 %copy-done.6 = bf16[112,384]{1,0:T(8,128)(2,1)S(1)} copy-done((bf16[112,384]{1,0:T(8,128)(2,1)S(1)}, bf16[112,384]{1,0:T(8,128)(2,1)}, u32[]{:S(2)}) %copy-start.6) | copy-done | bytes 86040
  4.5 0.0 copy-start.8
  4.5 0.7 copy-done.8
  5.2 0.0 copy-start.9
  5.2 0.7 copy-done.9
  5.8 0.0 copy-start.2
  5.8 0.0 copy-start.7
  5.9 11.2 %local_reductions.1 = (f32[16,40,128]{2,1,0:T(8,128)S(1)}, f32[16,40,128]{2,1,0:T(8,128)S(1)}, f32[112,128]{1,0:T(8,128)S(1)}) custom-call(s32[1]{0:T(128)} %bitcast.core_ref, bf16[128,112,128]{2,1,0:T(8,128)(2,1)S(1)} %copy-done, bf16[128,112,128]{2,1,0:T(8,128)(2,1)} %prev_ref.4, s32[5,128]{1,0:T(8,128)S(1)} %copy-done.8, s32[5,112]{1,0:T(8,128)S(1)} %copy-done.9, ...), custom_call_target="tpu_custom_call" | custom-call | tf_op jit(solution)/shard_map/local_reductions/pallas_call | solution.py:134
  17.1 3.3 %collective-permute-start = (f32[16,40,128]{2,1,0:T(8,128)S(1)}, f32[16,40,128]{2,1,0:T(8,128)S(1)}, u32[]{:S(2)}, u32[]{:S(2)}) collective-permute-start(f32[16,40,128]{2,1,0:T(8,128)S(1)} %get-tuple-element.28), channel_id=1, source_target_pairs={{0,1},{1,0},{2,3},{3,2},{4,5},{5,4},{6,7},{7,6},{8,9},{9,8},{10,11... | collective-permute-start | bytes 983048 | tf_op jit(solution)/shard_map/ppermute | solution.py:245
  20.4 1.3 %collective-permute-done = f32[16,40,128]{2,1,0:T(8,128)S(1)} collective-permute-done((f32[16,40,128]{2,1,0:T(8,128)S(1)}, f32[16,40,128]{2,1,0:T(8,128)S(1)}, u32[]{:S(2)}, u32[]{:S(2)}) %collective-permute-start) | collective-permute-done | bytes 327712 | tf_op jit(solution)/shard_map/ppermute | solution.py:245
  21.7 17.7 %all_to_all.10 = f32[16,40,128]{2,1,0:T(8,128)S(1)} all-to-all(f32[16,40,128]{2,1,0:T(8,128)S(1)} %add.18), channel_id=1, replica_groups=mesh['zh'=2,'x'=4,'y'=4,'zl'=4,'c'=2] {'y','zl'}, dimensions={0} | all-to-all | bytes 655360 | tf_op jit(solution)/shard_map/all_to_all | solution.py:253
  39.5 1.3 %collective-permute-start.1 = (f32[152,128]{1,0:T(8,128)S(1)}, f32[152,128]{1,0:T(8,128)S(1)}, u32[]{:S(2)}, u32[]{:S(2)}) collective-permute-start(f32[152,128]{1,0:T(8,128)S(1)} %pad_maximum_fusion), channel_id=1, source_target_pairs={{0,32},{32,0},{64,96},{96,64},{1,33},{33,1},{65,97},{97,65},{2,34}... | collective-permute-start | bytes 233480 | tf_op jit(solution)/shard_map/ppermute | solution.py:245
  40.8 2.0 %collective-permute-done.1 = f32[152,128]{1,0:T(8,128)S(1)} collective-permute-done((f32[152,128]{1,0:T(8,128)S(1)}, f32[152,128]{1,0:T(8,128)S(1)}, u32[]{:S(2)}, u32[]{:S(2)}) %collective-permute-start.1) | collective-permute-done | bytes 77856 | tf_op jit(solution)/shard_map/ppermute | solution.py:245
  42.8 2.6 %collective-permute-start.2 = (f32[152,128]{1,0:T(8,128)S(1)}, f32[152,128]{1,0:T(8,128)S(1)}, u32[]{:S(2)}, u32[]{:S(2)}) collective-permute-start(f32[152,128]{1,0:T(8,128)S(1)} %add.19), channel_id=1, source_target_pairs={{0,96},{32,64},{64,32},{96,0},{1,97},{33,65},{65,33},{97,1},{2,98}... | collective-permute-start | bytes 233480 | tf_op jit(solution)/shard_map/ppermute | solution.py:245
  45.4 0.0 copy-done.2
  45.4 0.0 copy-done.7
  45.4 0.0 copy-start.1
  45.4 2.0 %copy-done.1 = bf16[128,112,128]{2,1,0:T(8,128)(2,1)S(1)} copy-done((bf16[128,112,128]{2,1,0:T(8,128)(2,1)S(1)}, bf16[128,112,128]{2,1,0:T(8,128)(2,1)}, u32[]{:S(2)}) %copy-start.1) | copy-done | bytes 3670040
  47.4 4.0 %prev_grad.3.rest_0_ = bf16[128,112,128]{2,1,0:T(8,128)(2,1)} custom-call(bf16[128,112,128]{2,1,0:T(8,128)(2,1)S(1)} %copy-done.1, bf16[128,112,128]{2,1,0:T(8,128)(2,1)} %prev_ref.4, bf16[128,128]{1,0:T(8,128)(2,1)S(1)} %copy-done.2, f32[1,128]{1,0:T(1,128)S(1)} %bitcast.5), custom_call_target="tpu_custom_call" | custom-call | flops 587202560 | bytes 2752512 | tf_op jit(solution)/shard_map/prev_grad/pallas_call | solution.py:185
  51.4 0.0 collective-permute-done.2
  51.5 4.3 %collective-permute-start.3 = (f32[152,128]{1,0:T(8,128)S(1)}, f32[152,128]{1,0:T(8,128)S(1)}, u32[]{:S(2)}, u32[]{:S(2)}) collective-permute-start(f32[152,128]{1,0:T(8,128)S(1)} %add.20), channel_id=1, source_target_pairs={{0,128},{128,0},{1,129},{129,1},{2,130},{130,2},{3,131},{131,3},{4... | collective-permute-start | bytes 233480 | tf_op jit(solution)/shard_map/ppermute | solution.py:245
  55.8 5.2 %prev_grad.4.rest_0_ = bf16[128,112,128]{2,1,0:T(8,128)(2,1)} custom-call(bf16[128,112,128]{2,1,0:T(8,128)(2,1)S(1)} %copy-done.1, bf16[128,112,128]{2,1,0:T(8,128)(2,1)} %prev_ref.4, bf16[128,128]{1,0:T(8,128)(2,1)S(1)} %copy-done.2, f32[1,128]{1,0:T(1,128)S(1)} %bitcast.6, bf16[128,112,128]{2,1,0:T(8,128)(2,1)} %prev_grad.3.rest_0_), custom_call_target="tpu_custom_call", output_to_operand_aliasing={{}: (4, {})} | custom-call | flops 880803840 | bytes 4128768 | tf_op jit(solution)/shard_map/prev_grad/pallas_call | solution.py:185
  60.9 0.0 collective-permute-done.3
  60.9 0.1 slice_select_fusion
  61.1 12.5 %all_to_all.11.own_ref = f32[16,40,128]{2,1,0:T(8,128)S(1)} all-to-all(f32[16,40,128]{2,1,0:T(8,128)S(1)} %broadcast_in_dim.15), channel_id=1, replica_groups=mesh['zh'=2,'x'=4,'y'=4,'zl'=4,'c'=2] {'y','zl'}, dimensions={0} | all-to-all | bytes 655360 | tf_op jit(solution)/shard_map/all_to_all | solution.py:269
  73.5 0.0 copy-start.4
  73.5 0.0 copy-start.5
  73.5 0.0 copy-start.10
  73.5 4.4 %collective-permute-start.4 = (f32[16,40,128]{2,1,0:T(8,128)S(1)}, f32[16,40,128]{2,1,0:T(8,128)S(1)}, u32[]{:S(2)}, u32[]{:S(2)}) collective-permute-start(f32[16,40,128]{2,1,0:T(8,128)S(1)} %all_to_all.11.own_ref), channel_id=1, source_target_pairs={{0,1},{1,0},{2,3},{3,2},{4,5},{5,4},{6,7},{7,6},{8,9},{9,8},{10,11... | collective-permute-start | bytes 983048 | tf_op jit(solution)/shard_map/ppermute | solution.py:245
  78.0 5.2 %prev_grad.5 = bf16[128,112,128]{2,1,0:T(8,128)(2,1)} custom-call(bf16[128,112,128]{2,1,0:T(8,128)(2,1)S(1)} %copy-done.1, bf16[128,112,128]{2,1,0:T(8,128)(2,1)} %prev_ref.4, bf16[128,128]{1,0:T(8,128)(2,1)S(1)} %copy-done.2, f32[1,128]{1,0:T(1,128)S(1)} %bitcast.7, bf16[128,112,128]{2,1,0:T(8,128)(2,1)} %prev_grad.4.rest_0_), custom_call_target="tpu_custom_call", output_to_operand_aliasing={{}: (4, {})} | custom-call | flops 880803840 | bytes 4128768 | tf_op jit(solution)/shard_map/prev_grad/pallas_call | solution.py:185
  83.1 0.0 collective-permute-done.4.other_ref
  83.2 0.0 copy-done.4
  83.2 0.0 copy-done.5
  83.2 0.0 copy-done.10
  83.2 1.2 %finish.1 = (f32[128,384]{1,0:T(8,128)}, f32[112,384]{1,0:T(8,128)}, f32[384,128]{1,0:T(8,128)}, f32[384,128]{1,0:T(8,128)}, f32[128,128]{1,0:T(8,128)}, /*index...) custom-call(s32[1]{0:T(128)} %bitcast.core_ref, f32[16,40,128]{2,1,0:T(8,128)S(1)} %all_to_all.11.own_ref, ...), custom_call_target="tpu_custom_call" | custom-call | tf_op jit(solution)/shard_map/finish/pallas_call | solution.py:228
  (9 shorter events, 0.1 us)
Async XLA Ops:
  0.6 2.0 %copy-start = (bf16[128,112,128]{2,1,0:T(8,128)(2,1)S(1)}, bf16[128,112,128]{2,1,0:T(8,128)(2,1)}, u32[]{:S(2)}) copy-start(bf16[128,112,128]{2,1,0:T(8,128)(2,1)} %cot_ref.4) | copy-start | bytes 11010052
  2.7 0.9 %copy-start.3 = (bf16[128,384]{1,0:T(8,128)(2,1)S(1)}, bf16[128,384]{1,0:T(8,128)(2,1)}, u32[]{:S(2)}) copy-start(bf16[128,384]{1,0:T(8,128)(2,1)} %sr_ref.1) | copy-start | bytes 294916
  3.6 0.9 %copy-start.6 = (bf16[112,384]{1,0:T(8,128)(2,1)S(1)}, bf16[112,384]{1,0:T(8,128)(2,1)}, u32[]{:S(2)}) copy-start(bf16[112,384]{1,0:T(8,128)(2,1)} %sc_ref.1) | copy-start | bytes 258052
  4.5 0.7 copy-start.8
  5.2 0.7 copy-start.9
  5.8 39.5 %copy-start.2 = (bf16[128,128]{1,0:T(8,128)(2,1)S(1)}, bf16[128,128]{1,0:T(8,128)(2,1)}, u32[]{:S(2)}) copy-start(bf16[128,128]{1,0:T(8,128)(2,1)} %w_ref.7) | copy-start | bytes 98308
  5.8 39.5 %copy-start.7 = (f32[128]{0:T(128)S(1)}, f32[128]{0:T(128)}, u32[]{:S(2)}) copy-start(f32[128]{0:T(128)} %param.18) | copy-start | bytes 1540
  17.1 4.6 %collective-permute-start = (f32[16,40,128]{2,1,0:T(8,128)S(1)}, f32[16,40,128]{2,1,0:T(8,128)S(1)}, u32[]{:S(2)}, u32[]{:S(2)}) collective-permute-start(f32[16,40,128]{2,1,0:T(8,128)S(1)} %get-tuple-element.28), channel_id=1, source_target_pairs={{0,1},{1,0},{2,3},{3,2},{4,5},{5,4},{6,7},{7,6},{8,9},{9,8},{10,11... | collective-permute-start | bytes 983048 | tf_op jit(solution)/shard_map/ppermute | solution.py:245
  39.5 3.3 %collective-permute-start.1 = (f32[152,128]{1,0:T(8,128)S(1)}, f32[152,128]{1,0:T(8,128)S(1)}, u32[]{:S(2)}, u32[]{:S(2)}) collective-permute-start(f32[152,128]{1,0:T(8,128)S(1)} %pad_maximum_fusion), channel_id=1, source_target_pairs={{0,32},{32,0},{64,96},{96,64},{1,33},{33,1},{65,97},{97,65},{2,34}... | collective-permute-start | bytes 233480 | tf_op jit(solution)/shard_map/ppermute | solution.py:245
  42.8 8.6 %collective-permute-start.2 = (f32[152,128]{1,0:T(8,128)S(1)}, f32[152,128]{1,0:T(8,128)S(1)}, u32[]{:S(2)}, u32[]{:S(2)}) collective-permute-start(f32[152,128]{1,0:T(8,128)S(1)} %add.19), channel_id=1, source_target_pairs={{0,96},{32,64},{64,32},{96,0},{1,97},{33,65},{65,33},{97,1},{2,98}... | collective-permute-start | bytes 233480 | tf_op jit(solution)/shard_map/ppermute | solution.py:245
  45.4 2.0 %copy-start.1 = (bf16[128,112,128]{2,1,0:T(8,128)(2,1)S(1)}, bf16[128,112,128]{2,1,0:T(8,128)(2,1)}, u32[]{:S(2)}) copy-start(bf16[128,112,128]{2,1,0:T(8,128)(2,1)} %cot_ref.4) | copy-start | bytes 11010052
  51.5 9.5 %collective-permute-start.3 = (f32[152,128]{1,0:T(8,128)S(1)}, f32[152,128]{1,0:T(8,128)S(1)}, u32[]{:S(2)}, u32[]{:S(2)}) collective-permute-start(f32[152,128]{1,0:T(8,128)S(1)} %add.20), channel_id=1, source_target_pairs={{0,128},{128,0},{1,129},{129,1},{2,130},{130,2},{3,131},{131,3},{4... | collective-permute-start | bytes 233480 | tf_op jit(solution)/shard_map/ppermute | solution.py:245
  73.5 9.6 %copy-start.4 = (bf16[384,128]{1,0:T(8,128)(2,1)S(1)}, bf16[384,128]{1,0:T(8,128)(2,1)}, u32[]{:S(2)}) copy-start(bf16[384,128]{1,0:T(8,128)(2,1)} %wr_ref.1) | copy-start | bytes 294916
  73.5 9.6 %copy-start.5 = (bf16[384,128]{1,0:T(8,128)(2,1)S(1)}, bf16[384,128]{1,0:T(8,128)(2,1)}, u32[]{:S(2)}) copy-start(bf16[384,128]{1,0:T(8,128)(2,1)} %wc_ref.1) | copy-start | bytes 294916
  73.5 9.7 %copy-start.10 = (f32[128]{0:T(128)S(1)}, f32[128]{0:T(128)}, u32[]{:S(2)}) copy-start(f32[128]{0:T(128)} %param.19) | copy-start | bytes 1540
  73.5 9.6 %collective-permute-start.4 = (f32[16,40,128]{2,1,0:T(8,128)S(1)}, f32[16,40,128]{2,1,0:T(8,128)S(1)}, u32[]{:S(2)}, u32[]{:S(2)}) collective-permute-start(f32[16,40,128]{2,1,0:T(8,128)S(1)} %all_to_all.11.own_ref), channel_id=1, source_target_pairs={{0,1},{1,0},{2,3},{3,2},{4,5},{5,4},{6,7},{7,6},{8,9},{9,8},{10,11... | collective-permute-start | bytes 983048 | tf_op jit(solution)/shard_map/ppermute | solution.py:245

commit v2 on v1

v2 whole, which is shorter than its diff:
```python
import functools

import jax
import jax.numpy as jnp
from jax import lax
from jax.experimental import pallas as pl
from jax.experimental.pallas import tpu as pltpu
from jax.sharding import Mesh, PartitionSpec as P

F32, BF16 = jnp.float32, jnp.bfloat16
C = 128
S = 384
BINS = 139
SUB = 16
CHUNK = 40
PARTS = 32
VMEM = 60 * 1024 * 1024
ROW = ("zh", "x")
COLG = ("y", "zl")


def dot(a, b, dims):
    return lax.dot_general(a, b, (dims, ((), ())), preferred_element_type=F32)


def split_dot(a, b, dims, split_left):
    x = a if split_left else b
    hi = x.astype(BF16)
    rest = x - hi.astype(F32)
    mid = rest.astype(BF16)
    low = (rest - mid.astype(F32)).astype(BF16)
    if split_left:
        return dot(hi, b, dims) + (dot(mid, b, dims) + dot(low, b, dims))
    return dot(a, hi, dims) + (dot(a, mid, dims) + dot(a, low, dims))


def reduce_kernel(cols, steps, rows, core_ref, cot_ref, prev_ref, w_ref, gain_ref, bias_ref, idr_ref, idc_ref, sr_hbm, sc_hbm,
                  send_ref, keep_ref, colp_ref, dprev_ref, acc, gains, gcol, bcol, rowp, colp, buf, sr_ref, sc_ref, sems):
    step = pl.program_id(0)
    fetch = [pltpu.make_async_copy(sr_hbm, sr_ref, sems.at[0]), pltpu.make_async_copy(sc_hbm, sc_ref, sems.at[1])]

    @pl.when(step == 0)
    def _():
        acc[...] = jnp.zeros_like(acc)
        gains[...] = jnp.zeros_like(gains)
        gcol[...] = jnp.transpose(jnp.broadcast_to(gain_ref[...], (C, C)))
        bcol[...] = jnp.transpose(jnp.broadcast_to(bias_ref[...], (C, C)))
        colp[...] = jnp.zeros_like(colp)
        for f in fetch:
            f.start()

    n = SUB * cols
    idr = idr_ref[...].astype(F32)
    idc = idc_ref[...].astype(F32)
    gain, bias = gcol[:, 0:1], bcol[:, 0:1]
    lane = lax.broadcasted_iota(jnp.int32, (SUB, idr.shape[1]), 1)
    sub = lax.broadcasted_iota(jnp.int32, (SUB, idr.shape[1]), 0)
    flat_lane = lax.broadcasted_iota(jnp.int32, (16, n), 1)
    flat_sub = lax.broadcasted_iota(jnp.int32, (16, n), 0)
    rowind = jnp.where((flat_lane >= flat_sub * cols) & (flat_lane < (flat_sub + 1) * cols), 1.0, 0.0).astype(BF16)

    def mean(a):
        return jnp.sum(a, axis=0, keepdims=True) * (1.0 / C)

    for b in range(0, rows, SUB):
        first = step * rows + b
        cot = cot_ref[b:b + SUB].reshape(n, C)
        x = jnp.transpose(prev_ref[b:b + SUB].reshape(n, C)).astype(F32)
        centered = x - mean(x)
        rstd = lax.rsqrt(mean(centered * centered) + 1e-05)
        xhat = centered * rstd
        normed = (xhat * gain + bias).astype(BF16)
        g = dot(w_ref[...], cot, ((1,), (1,))) * gain
        gx = g * xhat
        share = gx[:, 0:C]
        for lo in range(C, n, C):
            share += gx[:, lo:lo + C]
        gains[...] += share
        res = (rstd * (g - mean(g) - xhat * mean(gx))).astype(BF16)
        dprev_ref[b:b + SUB] = jnp.transpose(res).reshape(SUB, cols, C)
        mask = lane == sub + first
        di = [jnp.sum(jnp.where(mask, idr[k:k + 1], 0.0), axis=1, keepdims=True) for k in range(5)]
        dj = [idc[k:k + 1] for k in range(5)]
        same_chain = di[2] == dj[2]
        same_res = same_chain & (di[0] == dj[0])
        same_entity = di[3] == dj[3]
        r = jnp.where(same_chain, jnp.clip(di[0] - dj[0] + 32.0, 0.0, 64.0), 65.0)
        t = jnp.where(same_res, jnp.clip(di[1] - dj[1] + 32.0, 0.0, 64.0), 65.0) + 66.0
        e = jnp.where(same_entity, 132.0, -1.0)
        c = jnp.where(same_entity & jnp.logical_not(same_chain), jnp.clip(di[4] - dj[4] + 2.0, 0.0, 4.0), 5.0) + 133.0
        r, t, e, c = [jnp.concatenate([v[s:s + 1] for s in range(SUB)], axis=1) for v in (r, t, e, c)]

        def hot(lo, hi, *codes):
            q = lax.broadcasted_iota(jnp.int32, (hi - lo, n), 0).astype(F32) + float(lo)
            hit = q == codes[0]
            for code in codes[1:]:
                hit = hit | (q == code)
            return jnp.where(hit, 1.0, 0.0).astype(BF16)

        left = jnp.concatenate(
            [normed, hot(0, 64, r), hot(64, 80, r, t), hot(80, 128, t), hot(128, 144, t, e, c), rowind], axis=0
        )
        out = dot(left, cot, ((1,), (0,)))
        acc[...] += out[:272]
        rowp[pl.ds(pl.multiple_of(first, SUB), SUB), :] = out[272:288]
        wide = cot_ref[b].astype(F32)
        for s in range(1, SUB):
            wide += cot_ref[b + s].astype(F32)
        colp[...] += wide

    @pl.when(step == steps - 1)
    def _():
        for f in fetch:
            f.wait()
        dwr = split_dot(sr_ref[...], rowp[...], ((0,), (0,)), False)
        dwc = split_dot(sc_ref[...], colp[...], ((0,), (0,)), False)
        acc[267:268] = jnp.sum(jnp.transpose(gains[...]), axis=0, keepdims=True) / gain_ref[...]
        total = acc[...]
        colp_ref[...] = colp[...]
        for k in range(PARTS):
            half, place = k // 16, k % 16
            buf[half, place, 0:4] = total[4 * k:4 * k + 4]
            buf[half, place, 4:8] = rowp[4 * k:4 * k + 4]
            lo, hi = 128 + 5 * k, min(128 + 5 * k + 5, 272)
            if lo < hi:
                buf[half, place, 8:8 + hi - lo] = total[lo:hi]
            pad = 8 + max(hi - lo, 0)
            buf[half, place, pad:16] = jnp.zeros((16 - pad, C), F32)
            buf[half, place, 16:28] = dwr[12 * k:12 * k + 12]
            buf[half, place, 28:40] = dwc[12 * k:12 * k + 12]
        core = core_ref[0]
        keep_ref[...] = buf[core]
        send_ref[...] = buf[1 - core]


def local_reductions(core, cot, prev, w, gain, bias, idr, idc, sr, sc, per=32):
    rows, cols = cot.shape[:2]
    steps = rows // per
    whole = lambda a: pl.BlockSpec(a.shape, lambda i: (0,) * a.ndim)
    block = pl.BlockSpec((per, cols, C), lambda i: (i, 0, 0))
    part = jax.ShapeDtypeStruct((16, CHUNK, C), F32)
    colo = jax.ShapeDtypeStruct((cols, C), F32)
    return pl.pallas_call(
        functools.partial(reduce_kernel, cols, steps, per),
        grid=(steps,),
        in_specs=[
            pl.BlockSpec(memory_space=pltpu.SMEM),
            block, block,
            whole(w), whole(gain), whole(bias), whole(idr), whole(idc),
            pl.BlockSpec(memory_space=pltpu.HBM), pl.BlockSpec(memory_space=pltpu.HBM),
        ],
        out_specs=[pl.BlockSpec(memory_space=pltpu.VMEM)] * 3 + [block],
        out_shape=[part, part, colo] + [jax.ShapeDtypeStruct(cot.shape, BF16)],
        scratch_shapes=[
            pltpu.VMEM((272, C), F32),
            pltpu.VMEM((C, C), F32),
            pltpu.VMEM((C, C), F32),
            pltpu.VMEM((C, C), F32),
            pltpu.VMEM((rows, C), F32),
            pltpu.VMEM((cols, C), F32),
            pltpu.VMEM((2, 16, CHUNK, C), F32),
            pltpu.VMEM(sr.shape, BF16),
            pltpu.VMEM(sc.shape, BF16),
            pltpu.SemaphoreType.DMA((2,)),
        ],
        compiler_params=pltpu.CompilerParams(vmem_limit_bytes=VMEM),
        name="local_reductions",
    )(core, cot, prev, w, gain, bias, idr, idc, sr, sc)


def final_kernel(core_ref, own_ref, other_ref, cols_ref, wr_ref, wc_ref, w_ref,
                 dsr_ref, dsc_ref, dwr_ref, dwc_ref, rec_ref, rel_ref, dg_ref, db_ref, buf, m, rows, rel):
    core = core_ref[0]
    buf[core] = own_ref[...]
    buf[1 - core] = other_ref[...]
    for k in range(PARTS):
        half, place = k // 16, k % 16
        m[4 * k:4 * k + 4] = buf[half, place, 0:4]
        rows[4 * k:4 * k + 4] = buf[half, place, 4:8]
        lo, hi = 5 * k, min(5 * k + 5, 144)
        if lo < hi:
            rel[lo:hi] = buf[half, place, 8:8 + hi - lo]
        dwr_ref[12 * k:12 * k + 12] = buf[half, place, 16:28]
        dwc_ref[12 * k:12 * k + 12] = buf[half, place, 28:40]
    rel_ref[...] = rel[0:BINS]
    total = jnp.sum(rel[133:139], axis=0, keepdims=True)
    big = m[...]
    w = w_ref[...].astype(F32)
    rec_ref[...] = big
    dg_ref[...] = rel[BINS:BINS + 1]
    db_ref[...] = jnp.sum(jnp.transpose(w * total), axis=0, keepdims=True)
    dsr_ref[...] = split_dot(rows[...], wr_ref[...], ((1,), (1,)), True)
    dsc_ref[...] = split_dot(cols_ref[...], wc_ref[...], ((1,), (1,)), True)


def finish(core, own, other, cols, wr, wc, w, nrows):
    f = lambda *s: jax.ShapeDtypeStruct(s, F32)
    vmem = pl.BlockSpec(memory_space=pltpu.VMEM)
    return pl.pallas_call(
        final_kernel,
        in_specs=[pl.BlockSpec(memory_space=pltpu.SMEM)] + [vmem] * 6,
        out_specs=[vmem] * 8,
        out_shape=[f(nrows, S), f(cols.shape[0], S), f(S, C), f(S, C), f(C, C), f(BINS, C), f(1, C), f(1, C)],
        scratch_shapes=[
            pltpu.VMEM((2, 16, CHUNK, C), F32),
            pltpu.VMEM((C, C), F32),
            pltpu.VMEM((nrows, C), F32),
            pltpu.VMEM((144, C), F32),
        ],
        compiler_params=pltpu.CompilerParams(vmem_limit_bytes=16 * 1024 * 1024),
        name="finish",
    )(core, own, other, cols, wr, wc, w)


def swap(a, axis, size, bit):
    return lax.ppermute(a, axis, [(i, i ^ bit) for i in range(size)])


def shards(cot, prev, single_rows, single_cols, w_row, w_col, w_rec, gain, bias, ids_rows, ids_cols):
    core = lax.axis_index("c").astype(jnp.int32).reshape(1)
    gain2, bias2 = gain.reshape(1, C), bias.reshape(1, C)
    send, keep, col_part, d_prev = local_reductions(
        core, cot, prev, w_rec, gain2, bias2, ids_rows, ids_cols, single_rows, single_cols
    )
    half = keep + swap(send, "c", 2, 1)
    chunks = lax.all_to_all(half, COLG, 0, 0)
    mine = jnp.sum(chunks, axis=0)
    z = jnp.concatenate([mine, col_part], axis=0)
    for axis, size, bit in (("x", 4, 1), ("x", 4, 3), ("zh", 2, 1)):
        z = z + swap(z, axis, size, bit)
    kept = lax.broadcasted_iota(jnp.int32, (CHUNK, 1), 0) // 4 == 1
    full = jnp.where(kept, mine, z[:CHUNK])
    col_sum = z[CHUNK:]
    own = lax.all_to_all(jnp.broadcast_to(full[None], (16, CHUNK, C)), COLG, 0, 0)
    other = swap(own, "c", 2, 1)
    dsr, dsc, dwr, dwc, rec, rel, dg, db = finish(core, own, other, col_sum, w_row, w_col, w_rec, cot.shape[0])
    return d_prev, dsr, dsc, dwr, dwc, rec, rel, dg.reshape(C), db.reshape(C)


def solution(mesh):
    fine = Mesh(mesh.devices.reshape(2, 4, 4, 4, 2), ("zh", "x", "y", "zl", "c"))
    row, col = ROW, COLG + ("c",)
    return jax.shard_map(
        shards,
        mesh=fine,
        in_specs=(
            P(row, col, None), P(row, col, None), P(row, None), P(col, None),
            P(), P(), P(), P(), P(), P(None, row), P(None, col),
        ),
        out_specs=(P(row, col, None), P(row, None), P(col, None), P(), P(), P(), P(), P(), P()),
        check_vma=False,
    )
```

time: 84.9 us -> 74.3 us (0.88)
  Pallas kernels: 26.8 us -> 13.2 us
  local copies, waits for them, and re-layouts: 7.27 us -> 0.05 us
  waiting for transfers between devices: 3.3 us -> 9.66 us
  other arithmetic: 0.18 us -> 2.81 us
  starting transfers between devices: 15.9 us -> 17.3 us
    pallas_call x3 -> x0, Pallas kernels: 14.4 us -> none  [prev_grad(): pl.pallas_call(functools.partial(prev_kernel, cols, per), grid=((hi - lo)...]
    unnamed x22 -> x6, local copies, waits for them, and re-layouts: 7.24 us -> 0.02 us
    ppermute x5, waiting for transfers between devices: 3.3 us -> 9.66 us  [swap(): return lax.ppermute(a, axis, [(i, i ^ bit) for i in range(size)])]
    ppermute x5, starting transfers between devices: 15.9 us -> 17.3 us  [swap(): return lax.ppermute(a, axis, [(i, i ^ bit) for i in range(size)])]
    add x1, other arithmetic: 0.03 us -> 1.02 us  [shards(): half = keep + swap(send, 'c', 2, 1)]
  transfers between devices with their start and end apart: 5 -> 5, of which waited for: 2 -> 5; matrix products, arithmetic and copies ran while one was open for 0% -> 0% of each run, Pallas kernels for 17% -> 0%
where the time goes in v2:
time: 74.3 us; the launch traced here: 74 us
  blocking collectives  30.2 us (41%)
  starting transfers between devices  17.3 us (23%)
  Pallas kernels  13.2 us (18%)
  waiting for transfers between devices  9.66 us (13%)
  other arithmetic  2.81 us (4%)
    all_to_all x1, blocking collectives, shards(): chunks = lax.all_to_all(half, COLG, 0, 0)  17.7 us
    ppermute x5, starting transfers between devices, swap(): return lax.ppermute(a, axis, [(i, i ^ bit) for i in range(size)])  17.3 us
    all_to_all x1, blocking collectives, shards(): lax.all_to_all(jnp.broadcast_to(full[None], (16, CHUNK, C)), COLG, 0, 0)  12.5 us
    pallas_call x1, Pallas kernels, local_reductions(): pl.pallas_call(functools.partial(reduce_kernel, cols, steps, per), grid=(...  12 us
    ppermute x5, waiting for transfers between devices, swap(): return lax.ppermute(a, axis, [(i, i ^ bit) for i in range(size)])  9.66 us
  transfers between devices with their start and end apart: 5, of which 5 were waited for; matrix products, arithmetic and copies ran while one was open for 0% of the time, Pallas kernels for 0%

profile of v2, /device:TPU:1, one launch (start us, length us, event | category | flops | bytes accessed | tf_op | source)
XLA Modules:
  0.0 74.0 jit_solution(9529558316693189762)
XLA Ops:
  0.6 12.0 %local_reductions.1 = (f32[16,40,128]{2,1,0:T(8,128)}, f32[16,40,128]{2,1,0:T(8,128)}, f32[112,128]{1,0:T(8,128)}, bf16[128,112,128]{2,1,0:T(8,128)(2,1)}) custom-call(s32[1]{0:T(128)} %bitcast.core_ref, bf16[128,112,128]{2,1,0:T(8,128)(2,1)} %cot_ref.1, bf16[128,112,128]{2,1,0:T(8,128)(2,1)} %prev_ref.1, bf16[128,128]{1,0:T(8,128)(2,1)} %w_ref.3, ...), custom_call_target="tpu_custom_call" | custom-call | tf_op jit(solution)/shard_map/local_reductions/pallas_call | solution.py:143
  12.6 0.0 copy-start
  12.7 0.0 copy-start.1
  12.7 0.0 copy-start.2
  12.7 3.3 %collective-permute-start = (f32[16,40,128]{2,1,0:T(8,128)}, f32[16,40,128]{2,1,0:T(8,128)S(1)}, u32[]{:S(2)}, u32[]{:S(2)}) collective-permute-start(f32[16,40,128]{2,1,0:T(8,128)} %get-tuple-element.23), channel_id=1, source_target_pairs={{0,1},{1,0},{2,3},{3,2},{4,5},{5,4},{6,7},{7,6},{8,9},{9,8},{10,11... | collective-permute-start | bytes 983048 | tf_op jit(solution)/shard_map/ppermute | solution.py:216
  16.0 1.5 %collective-permute-done = f32[16,40,128]{2,1,0:T(8,128)S(1)} collective-permute-done((f32[16,40,128]{2,1,0:T(8,128)}, f32[16,40,128]{2,1,0:T(8,128)S(1)}, u32[]{:S(2)}, u32[]{:S(2)}) %collective-permute-start) | collective-permute-done | bytes 327712 | tf_op jit(solution)/shard_map/ppermute | solution.py:216
  17.5 1.0 %add.18 = f32[16,40,128]{2,1,0:T(8,128)S(1)} add(f32[16,40,128]{2,1,0:T(8,128)} %get-tuple-element.22, f32[16,40,128]{2,1,0:T(8,128)S(1)} %collective-permute-done) | non-fusion elementwise | flops 81920 | bytes 983040 | tf_op jit(solution)/shard_map/add | solution.py:225
  18.5 17.7 %all_to_all.10 = f32[16,40,128]{2,1,0:T(8,128)S(1)} all-to-all(f32[16,40,128]{2,1,0:T(8,128)S(1)} %add.18), channel_id=1, replica_groups=mesh['zh'=2,'x'=4,'y'=4,'zl'=4,'c'=2] {'y','zl'}, dimensions={0} | all-to-all | bytes 655360 | tf_op jit(solution)/shard_map/all_to_all | solution.py:226
  36.3 0.8 %pad_maximum_fusion = f32[152,128]{1,0:T(8,128)S(1)} fusion(f32[112,128]{1,0:T(8,128)} %get-tuple-element.24, f32[40,128]{1,0:T(8,128)S(1)} %reduce_sum.9), kind=kLoop, calls=%fused_computation | loop fusion | flops 19456 | bytes 155648 | tf_op jit(solution)/shard_map/concatenate | solution.py:228
  37.1 1.2 %collective-permute-start.1 = (f32[152,128]{1,0:T(8,128)S(1)}, f32[152,128]{1,0:T(8,128)S(1)}, u32[]{:S(2)}, u32[]{:S(2)}) collective-permute-start(f32[152,128]{1,0:T(8,128)S(1)} %pad_maximum_fusion), channel_id=1, source_target_pairs={{0,32},{32,0},{64,96},{96,64},{1,33},{33,1},{65,97},{97,65},{2,34}... | collective-permute-start | bytes 233480 | tf_op jit(solution)/shard_map/ppermute | solution.py:216
  38.3 2.0 %collective-permute-done.1 = f32[152,128]{1,0:T(8,128)S(1)} collective-permute-done((f32[152,128]{1,0:T(8,128)S(1)}, f32[152,128]{1,0:T(8,128)S(1)}, u32[]{:S(2)}, u32[]{:S(2)}) %collective-permute-start.1) | collective-permute-done | bytes 77856 | tf_op jit(solution)/shard_map/ppermute | solution.py:216
  40.4 0.8 %fusion.1 = f32[152,128]{1,0:T(8,128)S(1)} fusion(f32[152,128]{1,0:T(8,128)S(1)} %collective-permute-done.1, f32[112,128]{1,0:T(8,128)} %get-tuple-element.24, f32[40,128]{1,0:T(8,128)S(1)} %reduce_sum.9), kind=kLoop, calls=%fused_computation.7 | loop fusion | flops 38912 | bytes 233472 | tf_op jit(solution)/shard_map/add | solution.py:230
  41.2 2.6 %collective-permute-start.2 = (f32[152,128]{1,0:T(8,128)S(1)}, f32[152,128]{1,0:T(8,128)S(1)}, u32[]{:S(2)}, u32[]{:S(2)}) collective-permute-start(f32[152,128]{1,0:T(8,128)S(1)} %fusion.1), channel_id=1, source_target_pairs={{0,96},{32,64},{64,32},{96,0},{1,97},{33,65},{65,33},{97,1},{2,98}... | collective-permute-start | bytes 233480 | tf_op jit(solution)/shard_map/ppermute | solution.py:216
  43.7 2.0 %collective-permute-done.2 = f32[152,128]{1,0:T(8,128)S(1)} collective-permute-done((f32[152,128]{1,0:T(8,128)S(1)}, f32[152,128]{1,0:T(8,128)S(1)}, u32[]{:S(2)}, u32[]{:S(2)}) %collective-permute-start.2) | collective-permute-done | bytes 77856 | tf_op jit(solution)/shard_map/ppermute | solution.py:216
  45.7 4.3 %collective-permute-start.3 = (f32[152,128]{1,0:T(8,128)S(1)}, f32[152,128]{1,0:T(8,128)S(1)}, u32[]{:S(2)}, u32[]{:S(2)}) collective-permute-start(f32[152,128]{1,0:T(8,128)S(1)} %add.20), channel_id=1, source_target_pairs={{0,128},{128,0},{1,129},{129,1},{2,130},{130,2},{3,131},{131,3},{4... | collective-permute-start | bytes 233480 | tf_op jit(solution)/shard_map/ppermute | solution.py:216
  50.0 2.9 %collective-permute-done.3 = f32[152,128]{1,0:T(8,128)S(1)} collective-permute-done((f32[152,128]{1,0:T(8,128)S(1)}, f32[152,128]{1,0:T(8,128)S(1)}, u32[]{:S(2)}, u32[]{:S(2)}) %collective-permute-start.3) | collective-permute-done | bytes 77856 | tf_op jit(solution)/shard_map/ppermute | solution.py:216
  53.0 0.1 slice_select_fusion
  53.1 12.5 %all_to_all.11.own_ref = f32[16,40,128]{2,1,0:T(8,128)S(1)} all-to-all(f32[16,40,128]{2,1,0:T(8,128)S(1)} %broadcast_in_dim.15), channel_id=1, replica_groups=mesh['zh'=2,'x'=4,'y'=4,'zl'=4,'c'=2] {'y','zl'}, dimensions={0} | all-to-all | bytes 655360 | tf_op jit(solution)/shard_map/all_to_all | solution.py:234
  65.6 5.9 %collective-permute-start.4 = (f32[16,40,128]{2,1,0:T(8,128)S(1)}, f32[16,40,128]{2,1,0:T(8,128)S(1)}, u32[]{:S(2)}, u32[]{:S(2)}) collective-permute-start(f32[16,40,128]{2,1,0:T(8,128)S(1)} %all_to_all.11.own_ref), channel_id=1, source_target_pairs={{0,1},{1,0},{2,3},{3,2},{4,5},{5,4},{6,7},{7,6},{8,9},{9,8},{10,11... | collective-permute-start | bytes 983048 | tf_op jit(solution)/shard_map/ppermute | solution.py:216
  71.5 1.3 %collective-permute-done.4.other_ref = f32[16,40,128]{2,1,0:T(8,128)S(1)} collective-permute-done((f32[16,40,128]{2,1,0:T(8,128)S(1)}, f32[16,40,128]{2,1,0:T(8,128)S(1)}, u32[]{:S(2)}, u32[]{:S(2)}) %collective-permute-start.4) | collective-permute-done | bytes 327712 | tf_op jit(solution)/shard_map/ppermute | solution.py:216
  72.7 0.0 copy-done
  72.7 0.0 copy-done.1
  72.7 0.0 copy-done.2
  72.8 1.2 %finish.1 = (f32[128,384]{1,0:T(8,128)}, f32[112,384]{1,0:T(8,128)}, f32[384,128]{1,0:T(8,128)}, f32[384,128]{1,0:T(8,128)}, f32[128,128]{1,0:T(8,128)}, /*index...) custom-call(s32[1]{0:T(128)} %bitcast.core_ref, f32[16,40,128]{2,1,0:T(8,128)S(1)} %all_to_all.11.own_ref, ...), custom_call_target="tpu_custom_call" | custom-call | tf_op jit(solution)/shard_map/finish/pallas_call | solution.py:199
  (6 shorter events, 0.1 us)
Async XLA Ops:
  12.6 60.1 %copy-start = (bf16[128,128]{1,0:T(8,128)(2,1)S(1)}, bf16[128,128]{1,0:T(8,128)(2,1)}, u32[]{:S(2)}) copy-start(bf16[128,128]{1,0:T(8,128)(2,1)} %w_ref.3) | copy-start | bytes 98308
  12.7 60.1 %copy-start.1 = (bf16[384,128]{1,0:T(8,128)(2,1)S(1)}, bf16[384,128]{1,0:T(8,128)(2,1)}, u32[]{:S(2)}) copy-start(bf16[384,128]{1,0:T(8,128)(2,1)} %wr_ref.1) | copy-start | bytes 294916
  12.7 60.1 %copy-start.2 = (bf16[384,128]{1,0:T(8,128)(2,1)S(1)}, bf16[384,128]{1,0:T(8,128)(2,1)}, u32[]{:S(2)}) copy-start(bf16[384,128]{1,0:T(8,128)(2,1)} %wc_ref.1) | copy-start | bytes 294916
  12.7 4.8 %collective-permute-start = (f32[16,40,128]{2,1,0:T(8,128)}, f32[16,40,128]{2,1,0:T(8,128)S(1)}, u32[]{:S(2)}, u32[]{:S(2)}) collective-permute-start(f32[16,40,128]{2,1,0:T(8,128)} %get-tuple-element.23), channel_id=1, source_target_pairs={{0,1},{1,0},{2,3},{3,2},{4,5},{5,4},{6,7},{7,6},{8,9},{9,8},{10,11... | collective-permute-start | bytes 983048 | tf_op jit(solution)/shard_map/ppermute | solution.py:216
  37.1 3.2 %collective-permute-start.1 = (f32[152,128]{1,0:T(8,128)S(1)}, f32[152,128]{1,0:T(8,128)S(1)}, u32[]{:S(2)}, u32[]{:S(2)}) collective-permute-start(f32[152,128]{1,0:T(8,128)S(1)} %pad_maximum_fusion), channel_id=1, source_target_pairs={{0,32},{32,0},{64,96},{96,64},{1,33},{33,1},{65,97},{97,65},{2,34}... | collective-permute-start | bytes 233480 | tf_op jit(solution)/shard_map/ppermute | solution.py:216
  41.2 4.5 %collective-permute-start.2 = (f32[152,128]{1,0:T(8,128)S(1)}, f32[152,128]{1,0:T(8,128)S(1)}, u32[]{:S(2)}, u32[]{:S(2)}) collective-permute-start(f32[152,128]{1,0:T(8,128)S(1)} %fusion.1), channel_id=1, source_target_pairs={{0,96},{32,64},{64,32},{96,0},{1,97},{33,65},{65,33},{97,1},{2,98}... | collective-permute-start | bytes 233480 | tf_op jit(solution)/shard_map/ppermute | solution.py:216
  45.7 7.2 %collective-permute-start.3 = (f32[152,128]{1,0:T(8,128)S(1)}, f32[152,128]{1,0:T(8,128)S(1)}, u32[]{:S(2)}, u32[]{:S(2)}) collective-permute-start(f32[152,128]{1,0:T(8,128)S(1)} %add.20), channel_id=1, source_target_pairs={{0,128},{128,0},{1,129},{129,1},{2,130},{130,2},{3,131},{131,3},{4... | collective-permute-start | bytes 233480 | tf_op jit(solution)/shard_map/ppermute | solution.py:216
  65.6 7.2 %collective-permute-start.4 = (f32[16,40,128]{2,1,0:T(8,128)S(1)}, f32[16,40,128]{2,1,0:T(8,128)S(1)}, u32[]{:S(2)}, u32[]{:S(2)}) collective-permute-start(f32[16,40,128]{2,1,0:T(8,128)S(1)} %all_to_all.11.own_ref), channel_id=1, source_target_pairs={{0,1},{1,0},{2,3},{3,2},{4,5},{5,4},{6,7},{7,6},{8,9},{9,8},{10,11... | collective-permute-start | bytes 983048 | tf_op jit(solution)/shard_map/ppermute | solution.py:216

commit v3 on v2

--- a/solution.py
+++ b/solution.py
@@ -14,7 +14,7 @@
 SUB = 16
 CHUNK = 40
 PARTS = 32
-VMEM = 60 * 1024 * 1024
+VMEM = 40 * 1024 * 1024
 ROW = ("zh", "x")
 COLG = ("y", "zl")
 
@@ -26,12 +26,10 @@
 def split_dot(a, b, dims, split_left):
     x = a if split_left else b
     hi = x.astype(BF16)
-    rest = x - hi.astype(F32)
-    mid = rest.astype(BF16)
-    low = (rest - mid.astype(F32)).astype(BF16)
+    low = (x - hi.astype(F32)).astype(BF16)
     if split_left:
-        return dot(hi, b, dims) + (dot(mid, b, dims) + dot(low, b, dims))
-    return dot(a, hi, dims) + (dot(a, mid, dims) + dot(a, low, dims))
+        return dot(hi, b, dims) + dot(low, b, dims)
+    return dot(a, hi, dims) + dot(a, low, dims)
 
 
 def reduce_kernel(cols, steps, rows, core_ref, cot_ref, prev_ref, w_ref, gain_ref, bias_ref, idr_ref, idc_ref, sr_hbm, sc_hbm,
@@ -59,24 +57,35 @@
     flat_sub = lax.broadcasted_iota(jnp.int32, (16, n), 0)
     rowind = jnp.where((flat_lane >= flat_sub * cols) & (flat_lane < (flat_sub + 1) * cols), 1.0, 0.0).astype(BF16)
 
+    eye = lax.broadcasted_iota(jnp.int32, (C, C), 0) == lax.broadcasted_iota(jnp.int32, (C, C), 1)
+    centering = (jnp.where(eye, 1.0, 0.0) - 1.0 / C).astype(BF16)
+
+    w = w_ref[...]
+    lead = jnp.sum(w.astype(F32) * gcol[...], axis=0, keepdims=True) * (1.0 / C)
+    lead_hi = lead.astype(BF16).astype(F32)
+    sub16 = lax.broadcasted_iota(jnp.int32, (16, C), 0)
+    extra = jnp.where(sub16 == 0, lead_hi, jnp.where(sub16 == 1, lead - lead_hi, 0.0))
+    wide_w = jnp.concatenate([w, extra.astype(BF16)], axis=0)
+
     def mean(a):
         return jnp.sum(a, axis=0, keepdims=True) * (1.0 / C)
 
     for b in range(0, rows, SUB):
         first = step * rows + b
         cot = cot_ref[b:b + SUB].reshape(n, C)
-        x = jnp.transpose(prev_ref[b:b + SUB].reshape(n, C)).astype(F32)
-        centered = x - mean(x)
+        centered = dot(centering, prev_ref[b:b + SUB].reshape(n, C), ((1,), (1,)))
         rstd = lax.rsqrt(mean(centered * centered) + 1e-05)
         xhat = centered * rstd
         normed = (xhat * gain + bias).astype(BF16)
-        g = dot(w_ref[...], cot, ((1,), (1,))) * gain
+        y = dot(wide_w, cot, ((1,), (1,)))
+        g = y[:C] * gain
+        g_mean = y[C:C + 1] + y[C + 1:C + 2]
         gx = g * xhat
         share = gx[:, 0:C]
         for lo in range(C, n, C):
             share += gx[:, lo:lo + C]
         gains[...] += share
-        res = (rstd * (g - mean(g) - xhat * mean(gx))).astype(BF16)
+        res = (rstd * (g - g_mean - xhat * mean(gx))).astype(BF16)
         dprev_ref[b:b + SUB] = jnp.transpose(res).reshape(SUB, cols, C)
         mask = lane == sub + first
         di = [jnp.sum(jnp.where(mask, idr[k:k + 1], 0.0), axis=1, keepdims=True) for k in range(5)]
@@ -85,13 +94,15 @@
         same_res = same_chain & (di[0] == dj[0])
         same_entity = di[3] == dj[3]
         r = jnp.where(same_chain, jnp.clip(di[0] - dj[0] + 32.0, 0.0, 64.0), 65.0)
-        t = jnp.where(same_res, jnp.clip(di[1] - dj[1] + 32.0, 0.0, 64.0), 65.0) + 66.0
-        e = jnp.where(same_entity, 132.0, -1.0)
-        c = jnp.where(same_entity & jnp.logical_not(same_chain), jnp.clip(di[4] - dj[4] + 2.0, 0.0, 4.0), 5.0) + 133.0
-        r, t, e, c = [jnp.concatenate([v[s:s + 1] for s in range(SUB)], axis=1) for v in (r, t, e, c)]
+        t = jnp.where(same_res, jnp.clip(di[1] - dj[1] + 32.0, 0.0, 64.0), 65.0)
+        c = jnp.where(same_entity & jnp.logical_not(same_chain), jnp.clip(di[4] - dj[4] + 2.0, 0.0, 4.0), 5.0)
+        packed = (r + 128.0 * t + 16384.0 * c).astype(jnp.int32) + jnp.where(same_entity, 1 << 18, 0)
+        packed = jnp.concatenate([packed[s:s + 1] for s in range(SUB)], axis=1)
+        r, t, c = packed & 127, ((packed >> 7) & 127) + 66, ((packed >> 14) & 15) + 133
+        e = jnp.where(packed >= 1 << 18, 132, -1)
 
         def hot(lo, hi, *codes):
-            q = lax.broadcasted_iota(jnp.int32, (hi - lo, n), 0).astype(F32) + float(lo)
+            q = lax.broadcasted_iota(jnp.int32, (hi - lo, n), 0) + lo
             hit = q == codes[0]
             for code in codes[1:]:
                 hit = hit | (q == code)
@@ -165,7 +176,7 @@
         ],
         compiler_params=pltpu.CompilerParams(vmem_limit_bytes=VMEM),
         name="local_reductions",
-    )(core, cot, prev, w, gain, bias, idr, idc, sr, sc)
+    )(core, *[pltpu.with_memory_space_constraint(a, pltpu.HBM) for a in (cot, prev, w, gain, bias, idr, idc, sr, sc)])
 
 
 def final_kernel(core_ref, own_ref, other_ref, cols_ref, wr_ref, wc_ref, w_ref,
@@ -226,8 +237,9 @@
     chunks = lax.all_to_all(half, COLG, 0, 0)
     mine = jnp.sum(chunks, axis=0)
     z = jnp.concatenate([mine, col_part], axis=0)
-    for axis, size, bit in (("x", 4, 1), ("x", 4, 3), ("zh", 2, 1)):
-        z = z + swap(z, axis, size, bit)
+    a, b, c = [swap(z, "x", 4, bit) for bit in (1, 3, 2)]
+    z = (z + a) + (c + b)
+    z = z + swap(z, "zh", 2, 1)
     kept = lax.broadcasted_iota(jnp.int32, (CHUNK, 1), 0) // 4 == 1
     full = jnp.where(kept, mine, z[:CHUNK])
     col_sum = z[CHUNK:]

time: 74.3 us -> 68.8 us (0.926)
  other arithmetic: 2.81 us -> 0.18 us
  Pallas kernels: 13.2 us -> 11.8 us
  starting transfers between devices: 17.3 us -> 16.5 us
    pallas_call x1, Pallas kernels: 12 us -> 10.7 us  [local_reductions(): pl.pallas_call(functools.partial(reduce_kernel, cols, steps, per), grid=(...]
    add x1, other arithmetic: 1.02 us -> 0.03 us  [shards(): half = keep + swap(send, 'c', 2, 1)]
    add x3 -> x2, other arithmetic: 0.85 us -> 0.03 us  [the longest x1 0.02 us: shards(): z = z + a + (c + b)]
    concatenate x1, other arithmetic: 0.83 us -> 0.01 us  [shards(): z = jnp.concatenate([mine, col_part], axis=0)]
    ppermute x5 -> x6, starting transfers between devices: 17.3 us -> 16.5 us  [swap(): return lax.ppermute(a, axis, [(i, i ^ bit) for i in range(size)])]
    all_to_all x1, blocking collectives: 12.5 us -> 11.7 us  [shards(): lax.all_to_all(jnp.broadcast_to(full[None], (16, CHUNK, C)), COLG, 0, 0)]
    ppermute x5 -> x6, waiting for transfers between devices: 9.66 us -> 9.8 us  [swap(): return lax.ppermute(a, axis, [(i, i ^ bit) for i in range(size)])]
  transfers between devices with their start and end apart: 5 -> 6, of which waited for: 5 -> 5; matrix products, arithmetic and copies ran while one was open for 0% -> 0% of each run, Pallas kernels for 0% -> 0%
where the time goes in v3:
time: 68.8 us; the launch traced here: 68.6 us
  blocking collectives  29.5 us (43%)
  starting transfers between devices  16.5 us (24%)
  Pallas kernels  11.8 us (17%)
  waiting for transfers between devices  9.8 us (14%)
  between operations  0.72 us (1%)
    all_to_all x1, blocking collectives, shards(): chunks = lax.all_to_all(half, COLG, 0, 0)  17.7 us
    ppermute x6, starting transfers between devices, swap(): return lax.ppermute(a, axis, [(i, i ^ bit) for i in range(size)])  16.5 us
    all_to_all x1, blocking collectives, shards(): lax.all_to_all(jnp.broadcast_to(full[None], (16, CHUNK, C)), COLG, 0, 0)  11.7 us
    pallas_call x1, Pallas kernels, local_reductions(): pl.pallas_call(functools.partial(reduce_kernel, cols, steps, per), grid=(...  10.7 us
    ppermute x6, waiting for transfers between devices, swap(): return lax.ppermute(a, axis, [(i, i ^ bit) for i in range(size)])  9.8 us
  transfers between devices with their start and end apart: 6, of which 5 were waited for; matrix products, arithmetic and copies ran while one was open for 0% of the time, Pallas kernels for 0%

profile of v3, /device:TPU:1, one launch (start us, length us, event | category | flops | bytes accessed | tf_op | source)
XLA Modules:
  0.0 68.6 jit_solution(3319276198665127390)
XLA Ops:
  0.6 10.7 %local_reductions.1 = (f32[16,40,128]{2,1,0:T(8,128)S(1)}, f32[16,40,128]{2,1,0:T(8,128)S(1)}, f32[112,128]{1,0:T(8,128)S(1)}, bf16[128,112,128]{2,1,0:T(8,128)(2,1)}) custom-call(s32[1]{0:T(128)} %bitcast.core_ref, bf16[128,112,128]{2,1,0:T(8,128)(2,1)} %cot_ref.1, bf16[128,112,128]{2,1,0:T(8,128)(2,1)} %prev_ref.1, bf16[128,128]{1,0:T(8,128)(2,1)} %w_ref.3, ...), custom_call_target="tpu_custom_call" | custom-call | tf_op jit(solution)/shard_map/local_reductions/pallas_call | solution.py:154
  11.3 0.0 copy-start
  11.3 0.0 copy-start.1
  11.3 0.0 copy-start.2
  11.4 3.3 %collective-permute-start = (f32[16,40,128]{2,1,0:T(8,128)S(1)}, f32[16,40,128]{2,1,0:T(8,128)S(1)}, u32[]{:S(2)}, u32[]{:S(2)}) collective-permute-start(f32[16,40,128]{2,1,0:T(8,128)S(1)} %get-tuple-element.23), channel_id=1, source_target_pairs={{0,1},{1,0},{2,3},{3,2},{4,5},{5,4},{6,7},{7,6},{8,9},{9,8},{10,11... | collective-permute-start | bytes 983048 | tf_op jit(solution)/shard_map/ppermute | solution.py:227
  14.7 1.3 %collective-permute-done = f32[16,40,128]{2,1,0:T(8,128)S(1)} collective-permute-done((f32[16,40,128]{2,1,0:T(8,128)S(1)}, f32[16,40,128]{2,1,0:T(8,128)S(1)}, u32[]{:S(2)}, u32[]{:S(2)}) %collective-permute-start) | collective-permute-done | bytes 327712 | tf_op jit(solution)/shard_map/ppermute | solution.py:227
  16.0 17.7 %all_to_all.10 = f32[16,40,128]{2,1,0:T(8,128)S(1)} all-to-all(f32[16,40,128]{2,1,0:T(8,128)S(1)} %add.21), channel_id=1, replica_groups=mesh['zh'=2,'x'=4,'y'=4,'zl'=4,'c'=2] {'y','zl'}, dimensions={0} | all-to-all | bytes 655360 | tf_op jit(solution)/shard_map/all_to_all | solution.py:237
  33.8 2.8 %collective-permute-start.2 = (f32[152,128]{1,0:T(8,128)S(1)}, f32[152,128]{1,0:T(8,128)S(1)}, u32[]{:S(2)}, u32[]{:S(2)}) collective-permute-start(f32[152,128]{1,0:T(8,128)S(1)} %pad_maximum_fusion), channel_id=1, source_target_pairs={{0,64},{32,96},{64,0},{96,32},{1,65},{33,97},{65,1},{97,33},{2,66}... | collective-permute-start | bytes 233480 | tf_op jit(solution)/shard_map/ppermute | solution.py:227
  36.6 0.9 %collective-permute-start.3 = (f32[152,128]{1,0:T(8,128)S(1)}, f32[152,128]{1,0:T(8,128)S(1)}, u32[]{:S(2)}, u32[]{:S(2)}) collective-permute-start(f32[152,128]{1,0:T(8,128)S(1)} %pad_maximum_fusion), channel_id=1, source_target_pairs={{0,96},{32,64},{64,32},{96,0},{1,97},{33,65},{65,33},{97,1},{2,98}... | collective-permute-start | bytes 233480 | tf_op jit(solution)/shard_map/ppermute | solution.py:227
  37.5 0.0 collective-permute-start.1
  37.5 1.1 %collective-permute-done.2 = f32[152,128]{1,0:T(8,128)S(1)} collective-permute-done((f32[152,128]{1,0:T(8,128)S(1)}, f32[152,128]{1,0:T(8,128)S(1)}, u32[]{:S(2)}, u32[]{:S(2)}) %collective-permute-start.2) | collective-permute-done | bytes 77856 | tf_op jit(solution)/shard_map/ppermute | solution.py:227
  38.6 3.2 %collective-permute-done.3 = f32[152,128]{1,0:T(8,128)S(1)} collective-permute-done((f32[152,128]{1,0:T(8,128)S(1)}, f32[152,128]{1,0:T(8,128)S(1)}, u32[]{:S(2)}, u32[]{:S(2)}) %collective-permute-start.3) | collective-permute-done | bytes 77856 | tf_op jit(solution)/shard_map/ppermute | solution.py:227
  41.8 0.0 collective-permute-done.1
  41.9 4.3 %collective-permute-start.4 = (f32[152,128]{1,0:T(8,128)S(1)}, f32[152,128]{1,0:T(8,128)S(1)}, u32[]{:S(2)}, u32[]{:S(2)}) collective-permute-start(f32[152,128]{1,0:T(8,128)S(1)} %add_add_fusion), channel_id=1, source_target_pairs={{0,128},{128,0},{1,129},{129,1},{2,130},{130,2},{3,131},{131,3},{4... | collective-permute-start | bytes 233480 | tf_op jit(solution)/shard_map/ppermute | solution.py:227
  46.2 2.9 %collective-permute-done.4 = f32[152,128]{1,0:T(8,128)S(1)} collective-permute-done((f32[152,128]{1,0:T(8,128)S(1)}, f32[152,128]{1,0:T(8,128)S(1)}, u32[]{:S(2)}, u32[]{:S(2)}) %collective-permute-start.4) | collective-permute-done | bytes 77856 | tf_op jit(solution)/shard_map/ppermute | solution.py:227
  49.1 0.1 slice_select_fusion
  49.2 11.7 %all_to_all.11.own_ref = f32[16,40,128]{2,1,0:T(8,128)S(1)} all-to-all(f32[16,40,128]{2,1,0:T(8,128)S(1)} %broadcast_in_dim.15), channel_id=1, replica_groups=mesh['zh'=2,'x'=4,'y'=4,'zl'=4,'c'=2] {'y','zl'}, dimensions={0} | all-to-all | bytes 655360 | tf_op jit(solution)/shard_map/all_to_all | solution.py:246
  60.9 5.2 %collective-permute-start.5 = (f32[16,40,128]{2,1,0:T(8,128)S(1)}, f32[16,40,128]{2,1,0:T(8,128)S(1)}, u32[]{:S(2)}, u32[]{:S(2)}) collective-permute-start(f32[16,40,128]{2,1,0:T(8,128)S(1)} %all_to_all.11.own_ref), channel_id=1, source_target_pairs={{0,1},{1,0},{2,3},{3,2},{4,5},{5,4},{6,7},{7,6},{8,9},{9,8},{10,11... | collective-permute-start | bytes 983048 | tf_op jit(solution)/shard_map/ppermute | solution.py:227
  66.1 1.3 %collective-permute-done.5.other_ref = f32[16,40,128]{2,1,0:T(8,128)S(1)} collective-permute-done((f32[16,40,128]{2,1,0:T(8,128)S(1)}, f32[16,40,128]{2,1,0:T(8,128)S(1)}, u32[]{:S(2)}, u32[]{:S(2)}) %collective-permute-start.5) | collective-permute-done | bytes 327712 | tf_op jit(solution)/shard_map/ppermute | solution.py:227
  67.4 0.0 copy-done
  67.4 0.0 copy-done.1
  67.4 0.0 copy-done.2
  67.4 1.2 %finish.1 = (f32[128,384]{1,0:T(8,128)}, f32[112,384]{1,0:T(8,128)}, f32[384,128]{1,0:T(8,128)}, f32[384,128]{1,0:T(8,128)}, f32[128,128]{1,0:T(8,128)}, /*index...) custom-call(s32[1]{0:T(128)} %bitcast.core_ref, f32[16,40,128]{2,1,0:T(8,128)S(1)} %all_to_all.11.own_ref, ...), custom_call_target="tpu_custom_call" | custom-call | tf_op jit(solution)/shard_map/finish/pallas_call | solution.py:210
  (8 shorter events, 0.1 us)
Async XLA Ops:
  11.3 56.1 %copy-start = (bf16[128,128]{1,0:T(8,128)(2,1)S(1)}, bf16[128,128]{1,0:T(8,128)(2,1)}, u32[]{:S(2)}) copy-start(bf16[128,128]{1,0:T(8,128)(2,1)} %w_ref.3) | copy-start | bytes 98308
  11.3 56.1 %copy-start.1 = (bf16[384,128]{1,0:T(8,128)(2,1)S(1)}, bf16[384,128]{1,0:T(8,128)(2,1)}, u32[]{:S(2)}) copy-start(bf16[384,128]{1,0:T(8,128)(2,1)} %wr_ref.1) | copy-start | bytes 294916
  11.3 56.0 %copy-start.2 = (bf16[384,128]{1,0:T(8,128)(2,1)S(1)}, bf16[384,128]{1,0:T(8,128)(2,1)}, u32[]{:S(2)}) copy-start(bf16[384,128]{1,0:T(8,128)(2,1)} %wc_ref.1) | copy-start | bytes 294916
  11.4 4.6 %collective-permute-start = (f32[16,40,128]{2,1,0:T(8,128)S(1)}, f32[16,40,128]{2,1,0:T(8,128)S(1)}, u32[]{:S(2)}, u32[]{:S(2)}) collective-permute-start(f32[16,40,128]{2,1,0:T(8,128)S(1)} %get-tuple-element.23), channel_id=1, source_target_pairs={{0,1},{1,0},{2,3},{3,2},{4,5},{5,4},{6,7},{7,6},{8,9},{9,8},{10,11... | collective-permute-start | bytes 983048 | tf_op jit(solution)/shard_map/ppermute | solution.py:227
  33.8 4.8 %collective-permute-start.2 = (f32[152,128]{1,0:T(8,128)S(1)}, f32[152,128]{1,0:T(8,128)S(1)}, u32[]{:S(2)}, u32[]{:S(2)}) collective-permute-start(f32[152,128]{1,0:T(8,128)S(1)} %pad_maximum_fusion), channel_id=1, source_target_pairs={{0,64},{32,96},{64,0},{96,32},{1,65},{33,97},{65,1},{97,33},{2,66}... | collective-permute-start | bytes 233480 | tf_op jit(solution)/shard_map/ppermute | solution.py:227
  36.6 5.2 %collective-permute-start.3 = (f32[152,128]{1,0:T(8,128)S(1)}, f32[152,128]{1,0:T(8,128)S(1)}, u32[]{:S(2)}, u32[]{:S(2)}) collective-permute-start(f32[152,128]{1,0:T(8,128)S(1)} %pad_maximum_fusion), channel_id=1, source_target_pairs={{0,96},{32,64},{64,32},{96,0},{1,97},{33,65},{65,33},{97,1},{2,98}... | collective-permute-start | bytes 233480 | tf_op jit(solution)/shard_map/ppermute | solution.py:227
  37.5 4.4 %collective-permute-start.1 = (f32[152,128]{1,0:T(8,128)S(1)}, f32[152,128]{1,0:T(8,128)S(1)}, u32[]{:S(2)}, u32[]{:S(2)}) collective-permute-start(f32[152,128]{1,0:T(8,128)S(1)} %pad_maximum_fusion), channel_id=1, source_target_pairs={{0,32},{32,0},{64,96},{96,64},{1,33},{33,1},{65,97},{97,65},{2,34}... | collective-permute-start | bytes 233480 | tf_op jit(solution)/shard_map/ppermute | solution.py:227
  41.9 7.2 %collective-permute-start.4 = (f32[152,128]{1,0:T(8,128)S(1)}, f32[152,128]{1,0:T(8,128)S(1)}, u32[]{:S(2)}, u32[]{:S(2)}) collective-permute-start(f32[152,128]{1,0:T(8,128)S(1)} %add_add_fusion), channel_id=1, source_target_pairs={{0,128},{128,0},{1,129},{129,1},{2,130},{130,2},{3,131},{131,3},{4... | collective-permute-start | bytes 233480 | tf_op jit(solution)/shard_map/ppermute | solution.py:227
  60.9 6.5 %collective-permute-start.5 = (f32[16,40,128]{2,1,0:T(8,128)S(1)}, f32[16,40,128]{2,1,0:T(8,128)S(1)}, u32[]{:S(2)}, u32[]{:S(2)}) collective-permute-start(f32[16,40,128]{2,1,0:T(8,128)S(1)} %all_to_all.11.own_ref), channel_id=1, source_target_pairs={{0,1},{1,0},{2,3},{3,2},{4,5},{5,4},{6,7},{7,6},{8,9},{9,8},{10,11... | collective-permute-start | bytes 983048 | tf_op jit(solution)/shard_map/ppermute | solution.py:227

commit v4 on v3

v4 whole, which is shorter than its diff:
```python
import functools

import jax
import jax.numpy as jnp
from jax import lax
from jax.experimental import pallas as pl
from jax.experimental.pallas import tpu as pltpu
from jax.sharding import Mesh, PartitionSpec as P

F32, BF16 = jnp.float32, jnp.bfloat16
C = 128
S = 384
BINS = 139
SUB = 16
CHUNK = 36
ROWS_AT, COLS_AT = 16, 28
WIDE = CHUNK + COLS_AT
PARTS = 32
PLANE, LINE = 16, 8
VMEM = 40 * 1024 * 1024
XY, Z = ("x", "y"), ("zh", "zl")
ROW, COL = ("zh", "x"), ("y", "zl", "c")


def dot(a, b, dims):
    return lax.dot_general(a, b, (dims, ((), ())), preferred_element_type=F32)


def split_dot(a, b, dims, split_left):
    x = a if split_left else b
    hi = x.astype(BF16)
    low = (x - hi.astype(F32)).astype(BF16)
    if split_left:
        return dot(hi, b, dims) + dot(low, b, dims)
    return dot(a, hi, dims) + dot(a, low, dims)


def reduce_kernel(cols, rows, cot_hbm, prev_hbm, w_hbm, gain_hbm, bias_hbm, idr_hbm, idc_hbm, sr_hbm, sc_hbm,
                  send_ref, keep_ref, colp_ref, dprev_hbm,
                  cot_ref, prev_ref, dprev_ref, w_ref, gain_ref, bias_ref, idr_ref, idc_ref, sr_ref, sc_ref,
                  acc, gains, gcol, bcol, rowp, buf, small_sems, in_sems, out_sems):
    units = rows // SUB
    small = [
        pltpu.make_async_copy(src, dst, small_sems.at[k])
        for k, (src, dst) in enumerate((
            (gain_hbm, gain_ref), (bias_hbm, bias_ref), (w_hbm, w_ref), (idr_hbm, idr_ref), (idc_hbm, idc_ref),
            (sr_hbm, sr_ref), (sc_hbm, sc_ref),
        ))
    ]

    def part(u):
        return pl.ds(pl.multiple_of(u * SUB, SUB), SUB)

    def fetch(u):
        return [
            pltpu.make_async_copy(src.at[part(u)], dst.at[part(u)], in_sems.at[k, u])
            for k, (src, dst) in enumerate(((prev_hbm, prev_ref), (cot_hbm, cot_ref)))
        ]

    def put(u):
        return pltpu.make_async_copy(dprev_ref.at[part(u)], dprev_hbm.at[part(u)], out_sems.at[u])

    for copy in small[:5] + fetch(0) + fetch(1) + small[5:]:
        copy.start()
    acc[...] = jnp.zeros_like(acc)
    gains[...] = jnp.zeros_like(gains)
    colp_ref[...] = jnp.zeros_like(colp_ref)
    for copy in small[:5]:
        copy.wait()
    gcol[...] = jnp.transpose(jnp.broadcast_to(gain_ref[...], (C, C)))
    bcol[...] = jnp.transpose(jnp.broadcast_to(bias_ref[...], (C, C)))

    n = SUB * cols
    idr = idr_ref[...].astype(F32)
    idc = idc_ref[...].astype(F32)
    gain, bias = gcol[:, 0:1], bcol[:, 0:1]
    lane = lax.broadcasted_iota(jnp.int32, (SUB, idr.shape[1]), 1)
    sub = lax.broadcasted_iota(jnp.int32, (SUB, idr.shape[1]), 0)
    flat_lane = lax.broadcasted_iota(jnp.int32, (16, n), 1)
    flat_sub = lax.broadcasted_iota(jnp.int32, (16, n), 0)
    rowind = jnp.where((flat_lane >= flat_sub * cols) & (flat_lane < (flat_sub + 1) * cols), 1.0, 0.0).astype(BF16)

    eye = lax.broadcasted_iota(jnp.int32, (C, C), 0) == lax.broadcasted_iota(jnp.int32, (C, C), 1)
    centering = (jnp.where(eye, 1.0, 0.0) - 1.0 / C).astype(BF16)

    w = w_ref[...]
    lead = jnp.sum(w.astype(F32) * gcol[...], axis=0, keepdims=True) * (1.0 / C)
    lead_hi = lead.astype(BF16).astype(F32)
    sub16 = lax.broadcasted_iota(jnp.int32, (16, C), 0)
    extra = jnp.where(sub16 == 0, lead_hi, jnp.where(sub16 == 1, lead - lead_hi, 0.0))
    wide_w = jnp.concatenate([w, extra.astype(BF16)], axis=0)

    def mean(a):
        return jnp.sum(a, axis=0, keepdims=True) * (1.0 / C)

    @pl.loop(0, units, unroll=8)
    def _(u):
        for copy in fetch(u):
            copy.wait()

        @pl.when(u + 2 < units)
        def _():
            for copy in fetch(u + 2):
                copy.start()

        first = u * SUB
        here = part(u)
        cot = cot_ref[here].reshape(n, C)
        centered = dot(centering, prev_ref[here].reshape(n, C), ((1,), (1,)))
        rstd = lax.rsqrt(mean(centered * centered) + 1e-05)
        xhat = centered * rstd
        normed = (xhat * gain + bias).astype(BF16)
        y = dot(wide_w, cot, ((1,), (1,)))
        g = y[:C] * gain
        g_mean = y[C:C + 1] + y[C + 1:C + 2]
        gx = g * xhat
        share = gx[:, 0:C]
        for lo in range(C, n, C):
            share += gx[:, lo:lo + C]
        gains[...] += share
        res = (rstd * (g - g_mean - xhat * mean(gx))).astype(BF16)
        dprev_ref[here] = jnp.transpose(res).reshape(SUB, cols, C)
        put(u).start()
        mask = lane == sub + first
        di = [jnp.sum(jnp.where(mask, idr[k:k + 1], 0.0), axis=1, keepdims=True) for k in range(5)]
        dj = [idc[k:k + 1] for k in range(5)]
        same_chain = di[2] == dj[2]
        same_res = same_chain & (di[0] == dj[0])
        same_entity = di[3] == dj[3]
        r = jnp.where(same_chain, jnp.clip(di[0] - dj[0] + 32.0, 0.0, 64.0), 65.0)
        t = jnp.where(same_res, jnp.clip(di[1] - dj[1] + 32.0, 0.0, 64.0), 65.0)
        c = jnp.where(same_entity & jnp.logical_not(same_chain), jnp.clip(di[4] - dj[4] + 2.0, 0.0, 4.0), 5.0)
        packed = (r + 128.0 * t + 16384.0 * c).astype(jnp.int32) + jnp.where(same_entity, 1 << 18, 0)
        packed = jnp.concatenate([packed[s:s + 1] for s in range(SUB)], axis=1)
        r, t, c = packed & 127, ((packed >> 7) & 127) + 66, ((packed >> 14) & 15) + 133
        e = jnp.where(packed >= 1 << 18, 132, -1)

        def hot(lo, hi, *codes):
            q = lax.broadcasted_iota(jnp.int32, (hi - lo, n), 0) + lo
            hit = q == codes[0]
            for code in codes[1:]:
                hit = hit | (q == code)
            return jnp.where(hit, 1.0, 0.0).astype(BF16)

        left = jnp.concatenate(
            [normed, hot(0, 64, r), hot(64, 80, r, t), hot(80, 128, t), hot(128, 144, t, e, c), rowind], axis=0
        )
        out = dot(left, cot, ((1,), (0,)))
        acc[...] += out[:272]
        rowp[here, :] = out[272:288]
        wide = cot[:cols].astype(F32)
        for s in range(1, SUB):
            wide += cot[s * cols:(s + 1) * cols].astype(F32)
        colp_ref[...] += wide

    for copy in small[5:]:
        copy.wait()
    dwr = split_dot(sr_ref[...], rowp[...], ((0,), (0,)), False)
    dwc = split_dot(sc_ref[...], colp_ref[...], ((0,), (0,)), False)
    acc[267:268] = jnp.sum(jnp.transpose(gains[...]), axis=0, keepdims=True) / gain_ref[...]
    total = acc[...]
    for k in range(PARTS):
        half, at = k // PLANE, k % PLANE * CHUNK
        buf[half, at:at + 12] = dwr[12 * k:12 * k + 12]
        buf[half, at + 12:at + 24] = dwc[12 * k:12 * k + 12]
        buf[half, at + 24:at + 28] = total[4 * k:4 * k + 4]
        lo, hi = 128 + 5 * k, min(128 + 5 * k + 5, 272)
        if lo < hi:
            buf[half, at + 28:at + 28 + hi - lo] = total[lo:hi]
        pad = 28 + max(hi - lo, 0)
        buf[half, at + pad:at + CHUNK] = jnp.zeros((CHUNK - pad, C), F32)
    for half in range(2):
        buf[half, PLANE * CHUNK:] = rowp[half * rows // 2:(half + 1) * rows // 2]
    core = lax.axis_index("c")
    keep_ref[...] = buf[core]
    send_ref[...] = buf[1 - core]

    @pl.loop(0, units)
    def _(u):
        put(u).wait()


def local_reductions(cot, prev, w, gain, bias, idr, idc, sr, sc):
    rows, cols = cot.shape[:2]
    units = rows // SUB
    part = jax.ShapeDtypeStruct((PLANE * CHUNK + rows // 2, C), F32)
    hbm, vmem = pl.BlockSpec(memory_space=pltpu.HBM), pl.BlockSpec(memory_space=pltpu.VMEM)
    same = lambda a: pltpu.VMEM(a.shape, a.dtype)
    arrays = (cot, prev, w, gain, bias, idr, idc, sr, sc)
    return pl.pallas_call(
        functools.partial(reduce_kernel, cols, rows),
        in_specs=[hbm] * 9,
        out_specs=[vmem, vmem, vmem, hbm],
        out_shape=[part, part, jax.ShapeDtypeStruct((cols, C), F32), jax.ShapeDtypeStruct(cot.shape, BF16)],
        scratch_shapes=[same(cot), same(prev), same(cot)] + [same(a) for a in arrays[2:]] + [
            pltpu.VMEM((272, C), F32),
            pltpu.VMEM((C, C), F32),
            pltpu.VMEM((C, C), F32),
            pltpu.VMEM((C, C), F32),
            pltpu.VMEM((rows, C), F32),
            pltpu.VMEM((2,) + part.shape, F32),
            pltpu.SemaphoreType.DMA((7,)),
            pltpu.SemaphoreType.DMA((2, units)),
            pltpu.SemaphoreType.DMA((units,)),
        ],
        compiler_params=pltpu.CompilerParams(vmem_limit_bytes=VMEM),
        name="local_reductions",
    )(*[pltpu.with_memory_space_constraint(a, pltpu.HBM) for a in arrays])


def plane_kernel(keep_ref, got_ref, colp_ref, out_ref, mine_ref):
    x, y = lax.axis_index("x"), lax.axis_index("y")
    for k in range(PLANE):
        out_ref[k, 0:CHUNK] = keep_ref[CHUNK * k:CHUNK * (k + 1)] + got_ref[CHUNK * k:CHUNK * (k + 1)]
        out_ref[k, CHUNK:] = jnp.zeros((COLS_AT, C), F32)
    for j in range(4):
        at = PLANE * CHUNK + ROWS_AT * j
        part = keep_ref[at:at + ROWS_AT] + got_ref[at:at + ROWS_AT]
        out_ref[4 * x + j, CHUNK:CHUNK + ROWS_AT] = part

        @pl.when(y == j)
        def _():
            mine_ref[...] = part

    for j in range(4):
        out_ref[4 * j + y, CHUNK:] = colp_ref[COLS_AT * j:COLS_AT * (j + 1)]


def line_kernel(r_ref, row_ref, out_ref, mine_ref):
    x, y, zh, zl = [lax.axis_index(a) for a in ("x", "y", "zh", "zl")]
    total = r_ref[0, 0:CHUNK]
    for k in range(1, PLANE):
        total += r_ref[k, 0:CHUNK]
    rows = jnp.zeros((ROWS_AT, C), F32)
    cols = jnp.zeros((COLS_AT, C), F32)
    for j in range(4):
        rows += jnp.where(j == y, row_ref[...], r_ref[4 * x + j, CHUNK:CHUNK + ROWS_AT])
        cols += r_ref[4 * j + y, CHUNK:]
    for k in range(LINE):
        out_ref[k, 0:CHUNK] = total
        out_ref[k, CHUNK:] = jnp.zeros((COLS_AT, C), F32)
    out_ref[4 * (1 - zh) + zl, CHUNK:] = cols
    for j in range(4):
        out_ref[4 * zh + j, CHUNK:CHUNK + ROWS_AT] = rows
    mine_ref[...] = cols


def spread_kernel(r_ref, col_ref, out_ref, mine_ref):
    x, y, zh, zl = [lax.axis_index(a) for a in ("x", "y", "zh", "zl")]
    total = r_ref[0, 0:CHUNK]
    for k in range(1, LINE):
        total += r_ref[k, 0:CHUNK]
    rows = r_ref[4 * zh, CHUNK:CHUNK + ROWS_AT]
    for j in range(1, 4):
        rows += r_ref[4 * zh + j, CHUNK:CHUNK + ROWS_AT]
    cols = col_ref[...] + r_ref[4 * (1 - zh) + zl, CHUNK:]
    for k in range(PLANE):
        out_ref[k, 0:CHUNK] = total
        out_ref[k, CHUNK:] = jnp.zeros((COLS_AT, C), F32)
    for j in range(4):
        out_ref[4 * j + y, CHUNK:] = cols
    for j in range(4):
        out_ref[4 * x + j, CHUNK:CHUNK + ROWS_AT] = rows
    mine_ref[...] = cols


def glue(kernel, name, parts, mine, *args):
    vmem = pl.BlockSpec(memory_space=pltpu.VMEM)
    return pl.pallas_call(
        kernel,
        in_specs=[vmem] * len(args),
        out_specs=[vmem] * 2,
        out_shape=[jax.ShapeDtypeStruct((parts, WIDE, C), F32), jax.ShapeDtypeStruct((mine, C), F32)],
        compiler_params=pltpu.CompilerParams(vmem_limit_bytes=16 * 1024 * 1024),
        name=name,
    )(*args)


def final_kernel(own_ref, other_ref, col_ref, wr_ref, wc_ref, w_ref,
                 dsr_ref, dsc_ref, dwr_ref, dwc_ref, rec_ref, rel_ref, dg_ref, db_ref, buf, m, rows, cols, rel):
    core, x, y = [lax.axis_index(a) for a in ("c", "x", "y")]
    buf[core] = own_ref[...]
    buf[1 - core] = other_ref[...]
    for k in range(PARTS):
        half, place = k // PLANE, k % PLANE
        dwr_ref[12 * k:12 * k + 12] = buf[half, place, 0:12]
        dwc_ref[12 * k:12 * k + 12] = buf[half, place, 12:24]
        m[4 * k:4 * k + 4] = buf[half, place, 24:28]
        lo, hi = 5 * k, min(5 * k + 5, 144)
        if lo < hi:
            rel[lo:hi] = buf[half, place, 28:28 + hi - lo]
    for half in range(2):
        for j in range(4):
            at = ROWS_AT * (4 * half + j)
            rows[at:at + ROWS_AT] = buf[half, 4 * x + j, CHUNK:CHUNK + ROWS_AT]
    for j in range(4):
        cols[COLS_AT * j:COLS_AT * (j + 1)] = jnp.where(j == x, col_ref[...], own_ref[4 * j + y, CHUNK:])
    rel_ref[...] = rel[0:BINS]
    total = jnp.sum(rel[133:139], axis=0, keepdims=True)
    w = w_ref[...].astype(F32)
    rec_ref[...] = m[...]
    dg_ref[...] = rel[BINS:BINS + 1]
    db_ref[...] = jnp.sum(jnp.transpose(w * total), axis=0, keepdims=True)
    dsr_ref[...] = split_dot(rows[...], wr_ref[...], ((1,), (1,)), True)
    dsc_ref[...] = split_dot(cols[...], wc_ref[...], ((1,), (1,)), True)


def finish(own, other, col, wr, wc, w, nrows, ncols):
    f = lambda *s: jax.ShapeDtypeStruct(s, F32)
    vmem = pl.BlockSpec(memory_space=pltpu.VMEM)
    return pl.pallas_call(
        final_kernel,
        in_specs=[vmem] * 6,
        out_specs=[vmem] * 8,
        out_shape=[f(nrows, S), f(ncols, S), f(S, C), f(S, C), f(C, C), f(BINS, C), f(1, C), f(1, C)],
        scratch_shapes=[
            pltpu.VMEM((2, PLANE, WIDE, C), F32),
            pltpu.VMEM((C, C), F32),
            pltpu.VMEM((nrows, C), F32),
            pltpu.VMEM((ncols, C), F32),
            pltpu.VMEM((144, C), F32),
        ],
        compiler_params=pltpu.CompilerParams(vmem_limit_bytes=16 * 1024 * 1024),
        name="finish",
    )(own, other, col, wr, wc, w)


def swap(a):
    return lax.ppermute(a, "c", [(0, 1), (1, 0)])


def shards(cot, prev, single_rows, single_cols, w_row, w_col, w_rec, gain, bias, ids_rows, ids_cols):
    nrows, ncols = cot.shape[:2]
    gain2, bias2 = gain.reshape(1, C), bias.reshape(1, C)
    send, keep, col_part, d_prev = local_reductions(
        cot, prev, w_rec, gain2, bias2, ids_rows, ids_cols, single_rows, single_cols
    )
    shares, row_mine = glue(plane_kernel, "plane", PLANE, ROWS_AT, keep, swap(send), col_part)
    shares, col_mine = glue(line_kernel, "line", LINE, COLS_AT, lax.all_to_all(shares, XY, 0, 0), row_mine)
    shares, col_mine = glue(spread_kernel, "spread", PLANE, COLS_AT, lax.all_to_all(shares, Z, 0, 0), col_mine)
    own = lax.all_to_all(shares, XY, 0, 0)
    dsr, dsc, dwr, dwc, rec, rel, dg, db = finish(own, swap(own), col_mine, w_row, w_col, w_rec, nrows, ncols)
    return d_prev, dsr, dsc, dwr, dwc, rec, rel, dg.reshape(C), db.reshape(C)


def solution(mesh):
    fine = Mesh(mesh.devices.reshape(2, 4, 4, 4, 2), ("zh", "x", "y", "zl", "c"))
    return jax.shard_map(
        shards,
        mesh=fine,
        in_specs=(
            P(ROW, COL, None), P(ROW, COL, None), P(ROW, None), P(COL, None),
            P(), P(), P(), P(), P(), P(None, ROW), P(None, COL),
        ),
        out_specs=(P(ROW, COL, None), P(ROW, None), P(COL, None), P(), P(), P(), P(), P(), P()),
        check_vma=False,
    )
```

time: 68.8 us -> 68.7 us (level)
  blocking collectives: 29.5 us -> 45.1 us
  starting transfers between devices: 16.5 us -> 8.11 us
  waiting for transfers between devices: 9.8 us -> 2.79 us
    all_to_all x2 -> x3, blocking collectives: 29.5 us -> 45.1 us  [the longest x1 17.4 us: shards(): lax.all_to_all(shares, Z, 0, 0)]
    ppermute x6 -> x2, starting transfers between devices: 16.5 us -> 8.11 us  [swap(): return lax.ppermute(a, 'c', [(0, 1), (1, 0)])]
    ppermute x6 -> x2, waiting for transfers between devices: 9.8 us -> 2.79 us  [swap(): return lax.ppermute(a, 'c', [(0, 1), (1, 0)])]
    pallas_call x2 -> x5, Pallas kernels: 11.8 us -> 11.8 us  [the longest x1 10.5 us: local_reductions(): pl.pallas_call(functools.partial(reduce_kernel, cols, rows), in_specs=[hb...]
  transfers between devices with their start and end apart: 6 -> 2, of which waited for: 5 -> 2; matrix products, arithmetic and copies ran while one was open for 0% -> 0% of each run, Pallas kernels for 0% -> 0%
where the time goes in v4:
time: 68.7 us; the launch traced here: 68.5 us
  blocking collectives  45.1 us (66%)
  Pallas kernels  11.8 us (17%)
  starting transfers between devices  8.11 us (12%)
  waiting for transfers between devices  2.79 us (4%)
  between operations  0.7 us (1%)
    all_to_all x1, blocking collectives, shards(): lax.all_to_all(shares, Z, 0, 0)  17.4 us
    all_to_all x1, blocking collectives, shards(): lax.all_to_all(shares, XY, 0, 0)  15.2 us
    all_to_all x1, blocking collectives, shards(): own = lax.all_to_all(shares, XY, 0, 0)  12.5 us
    pallas_call x1, Pallas kernels, local_reductions(): pl.pallas_call(functools.partial(reduce_kernel, cols, rows), in_specs=[hb...  10.5 us
    ppermute x2, starting transfers between devices, swap(): return lax.ppermute(a, 'c', [(0, 1), (1, 0)])  8.11 us
    ppermute x2, waiting for transfers between devices, swap(): return lax.ppermute(a, 'c', [(0, 1), (1, 0)])  2.79 us
  transfers between devices with their start and end apart: 2, of which 2 were waited for; matrix products, arithmetic and copies ran while one was open for 0% of the time, Pallas kernels for 0%

profile of v4, /device:TPU:1, one launch (start us, length us, event | category | flops | bytes accessed | tf_op | source)
XLA Modules:
  0.0 68.5 jit_solution(12054002730184971661)
XLA Ops:
  0.6 10.5 %local_reductions.1 = (f32[640,128]{1,0:T(8,128)S(1)}, f32[640,128]{1,0:T(8,128)S(1)}, f32[112,128]{1,0:T(8,128)S(1)}, bf16[128,112,128]{2,1,0:T(8,128)(2,1)}) custom-call(bf16[128,112,128]{2,1,0:T(8,128)(2,1)} %cot_hbm.1, bf16[128,112,128]{2,1,0:T(8,128)(2,1)} %prev_hbm.1, bf16[128,128]{1,0:T(8,128)(2,1)} %w_ref.1, f32[1,128]{1,0:T(1,128)} %bitcast.4, ...), custom_call_target="tpu_custom_call" | custom-call | tf_op jit(solution)/shard_map/local_reductions/pallas_call | solution.py:190
  11.1 0.0 copy-start
  11.1 0.0 copy-start.1
  11.2 0.0 copy-start.2
  11.2 3.3 %collective-permute-start = (f32[640,128]{1,0:T(8,128)S(1)}, f32[640,128]{1,0:T(8,128)S(1)}, u32[]{:S(2)}, u32[]{:S(2)}) collective-permute-start(f32[640,128]{1,0:T(8,128)S(1)} %get-tuple-element.29), channel_id=1, source_target_pairs={{0,1},{1,0},{2,3},{3,2},{4,5},{5,4},{6,7},{7,6},{8,9},{9,8},{10,11... | collective-permute-start | bytes 983048 | tf_op jit(solution)/shard_map/ppermute | solution.py:329
  14.5 1.3 %collective-permute-done.got_ref = f32[640,128]{1,0:T(8,128)S(1)} collective-permute-done((f32[640,128]{1,0:T(8,128)S(1)}, f32[640,128]{1,0:T(8,128)S(1)}, u32[]{:S(2)}, u32[]{:S(2)}) %collective-permute-start) | collective-permute-done | bytes 327712 | tf_op jit(solution)/shard_map/ppermute | solution.py:329
  15.8 0.1 plane.1
  15.8 15.2 %all_to_all.15.r_ref = f32[16,64,128]{2,1,0:T(8,128)S(1)} all-to-all(f32[16,64,128]{2,1,0:T(8,128)S(1)} %get-tuple-element.31), channel_id=1, replica_groups=mesh['zh'=2,'x'=4,'y'=4,'zl'=4,'c'=2] {'x','y'}, dimensions={0} | all-to-all | bytes 1048576 | tf_op jit(solution)/shard_map/all_to_all | solution.py:339
  31.0 17.4 %all_to_all.16.r_ref = f32[8,64,128]{2,1,0:T(8,128)S(1)} all-to-all(f32[8,64,128]{2,1,0:T(8,128)S(1)} %get-tuple-element.33), channel_id=1, replica_groups=mesh['zh'=2,'x'=4,'y'=4,'zl'=4,'c'=2] {'zh','zl'}, dimensions={0} | all-to-all | bytes 524288 | tf_op jit(solution)/shard_map/all_to_all | solution.py:340
  48.5 0.1 spread.1
  48.5 12.5 %all_to_all.17.own_ref = f32[16,64,128]{2,1,0:T(8,128)S(1)} all-to-all(f32[16,64,128]{2,1,0:T(8,128)S(1)} %get-tuple-element.35), channel_id=1, replica_groups=mesh['zh'=2,'x'=4,'y'=4,'zl'=4,'c'=2] {'x','y'}, dimensions={0} | all-to-all | bytes 1048576 | tf_op jit(solution)/shard_map/all_to_all | solution.py:341
  61.0 4.8 %collective-permute-start.1 = (f32[16,64,128]{2,1,0:T(8,128)S(1)}, f32[16,64,128]{2,1,0:T(8,128)S(1)}, u32[]{:S(2)}, u32[]{:S(2)}) collective-permute-start(f32[16,64,128]{2,1,0:T(8,128)S(1)} %all_to_all.17.own_ref), channel_id=1, source_target_pairs={{0,1},{1,0},{2,3},{3,2},{4,5},{5,4},{6,7},{7,6},{8,9},{9,8},{10,11... | collective-permute-start | bytes 1572872 | tf_op jit(solution)/shard_map/ppermute | solution.py:329
  65.8 1.5 %collective-permute-done.1.other_ref = f32[16,64,128]{2,1,0:T(8,128)S(1)} collective-permute-done((f32[16,64,128]{2,1,0:T(8,128)S(1)}, f32[16,64,128]{2,1,0:T(8,128)S(1)}, u32[]{:S(2)}, u32[]{:S(2)}) %collective-permute-start.1) | collective-permute-done | bytes 524320 | tf_op jit(solution)/shard_map/ppermute | solution.py:329
  67.4 0.0 copy-done
  67.4 0.0 copy-done.1
  67.4 0.0 copy-done.2
  67.4 1.2 %finish.1 = (f32[128,384]{1,0:T(8,128)}, f32[112,384]{1,0:T(8,128)}, f32[384,128]{1,0:T(8,128)}, f32[384,128]{1,0:T(8,128)}, f32[128,128]{1,0:T(8,128)}, /*index...) custom-call(f32[16,64,128]{2,1,0:T(8,128)S(1)} %all_to_all.17.own_ref, ...), custom_call_target="tpu_custom_call" | custom-call | tf_op jit(solution)/shard_map/finish/pallas_call | solution.py:311
  (1 shorter events, 0.0 us)
Async XLA Ops:
  11.1 56.2 %copy-start = (bf16[128,128]{1,0:T(8,128)(2,1)S(1)}, bf16[128,128]{1,0:T(8,128)(2,1)}, u32[]{:S(2)}) copy-start(bf16[128,128]{1,0:T(8,128)(2,1)} %w_ref.1) | copy-start | bytes 98308
  11.1 56.2 %copy-start.1 = (bf16[384,128]{1,0:T(8,128)(2,1)S(1)}, bf16[384,128]{1,0:T(8,128)(2,1)}, u32[]{:S(2)}) copy-start(bf16[384,128]{1,0:T(8,128)(2,1)} %wr_ref.1) | copy-start | bytes 294916
  11.2 56.2 %copy-start.2 = (bf16[384,128]{1,0:T(8,128)(2,1)S(1)}, bf16[384,128]{1,0:T(8,128)(2,1)}, u32[]{:S(2)}) copy-start(bf16[384,128]{1,0:T(8,128)(2,1)} %wc_ref.1) | copy-start | bytes 294916
  11.2 4.6 %collective-permute-start = (f32[640,128]{1,0:T(8,128)S(1)}, f32[640,128]{1,0:T(8,128)S(1)}, u32[]{:S(2)}, u32[]{:S(2)}) collective-permute-start(f32[640,128]{1,0:T(8,128)S(1)} %get-tuple-element.29), channel_id=1, source_target_pairs={{0,1},{1,0},{2,3},{3,2},{4,5},{5,4},{6,7},{7,6},{8,9},{9,8},{10,11... | collective-permute-start | bytes 983048 | tf_op jit(solution)/shard_map/ppermute | solution.py:329
  61.0 6.3 %collective-permute-start.1 = (f32[16,64,128]{2,1,0:T(8,128)S(1)}, f32[16,64,128]{2,1,0:T(8,128)S(1)}, u32[]{:S(2)}, u32[]{:S(2)}) collective-permute-start(f32[16,64,128]{2,1,0:T(8,128)S(1)} %all_to_all.17.own_ref), channel_id=1, source_target_pairs={{0,1},{1,0},{2,3},{3,2},{4,5},{5,4},{6,7},{7,6},{8,9},{9,8},{10,11... | collective-permute-start | bytes 1572872 | tf_op jit(solution)/shard_map/ppermute | solution.py:329

commit v5 on v4

--- a/solution.py
+++ b/solution.py
@@ -12,8 +12,9 @@
 S = 384
 BINS = 139
 SUB = 16
-CHUNK = 36
-ROWS_AT, COLS_AT = 16, 28
+SHARED = 33
+ROWS_AT, COLS_AT = 4, 7
+CHUNK = SHARED + ROWS_AT
 WIDE = CHUNK + COLS_AT
 PARTS = 32
 PLANE, LINE = 16, 8
@@ -167,10 +168,9 @@
         lo, hi = 128 + 5 * k, min(128 + 5 * k + 5, 272)
         if lo < hi:
             buf[half, at + 28:at + 28 + hi - lo] = total[lo:hi]
-        pad = 28 + max(hi - lo, 0)
-        buf[half, at + pad:at + CHUNK] = jnp.zeros((CHUNK - pad, C), F32)
-    for half in range(2):
-        buf[half, PLANE * CHUNK:] = rowp[half * rows // 2:(half + 1) * rows // 2]
+        if hi - lo < 5:
+            buf[half, at + 28 + max(hi - lo, 0):at + SHARED] = jnp.zeros((5 - max(hi - lo, 0), C), F32)
+        buf[half, at + SHARED:at + CHUNK] = rowp[ROWS_AT * k:ROWS_AT * (k + 1)]
     core = lax.axis_index("c")
     keep_ref[...] = buf[core]
     send_ref[...] = buf[1 - core]
@@ -183,7 +183,7 @@
 def local_reductions(cot, prev, w, gain, bias, idr, idc, sr, sc):
     rows, cols = cot.shape[:2]
     units = rows // SUB
-    part = jax.ShapeDtypeStruct((PLANE * CHUNK + rows // 2, C), F32)
+    part = jax.ShapeDtypeStruct((PLANE * CHUNK, C), F32)
     hbm, vmem = pl.BlockSpec(memory_space=pltpu.HBM), pl.BlockSpec(memory_space=pltpu.VMEM)
     same = lambda a: pltpu.VMEM(a.shape, a.dtype)
     arrays = (cot, prev, w, gain, bias, idr, idc, sr, sc)
@@ -208,77 +208,67 @@
     )(*[pltpu.with_memory_space_constraint(a, pltpu.HBM) for a in arrays])
 
 
-def plane_kernel(keep_ref, got_ref, colp_ref, out_ref, mine_ref):
-    x, y = lax.axis_index("x"), lax.axis_index("y")
+def plane_kernel(keep_ref, got_ref, colp_ref, out_ref):
     for k in range(PLANE):
-        out_ref[k, 0:CHUNK] = keep_ref[CHUNK * k:CHUNK * (k + 1)] + got_ref[CHUNK * k:CHUNK * (k + 1)]
-        out_ref[k, CHUNK:] = jnp.zeros((COLS_AT, C), F32)
-    for j in range(4):
-        at = PLANE * CHUNK + ROWS_AT * j
-        part = keep_ref[at:at + ROWS_AT] + got_ref[at:at + ROWS_AT]
-        out_ref[4 * x + j, CHUNK:CHUNK + ROWS_AT] = part
-
-        @pl.when(y == j)
-        def _():
-            mine_ref[...] = part
-
-    for j in range(4):
-        out_ref[4 * j + y, CHUNK:] = colp_ref[COLS_AT * j:COLS_AT * (j + 1)]
-
-
-def line_kernel(r_ref, row_ref, out_ref, mine_ref):
-    x, y, zh, zl = [lax.axis_index(a) for a in ("x", "y", "zh", "zl")]
-    total = r_ref[0, 0:CHUNK]
+        at = slice(CHUNK * k, CHUNK * (k + 1))
+        out_ref[k, 0:CHUNK] = keep_ref[at] + got_ref[at]
+        out_ref[k, CHUNK:] = colp_ref[COLS_AT * k:COLS_AT * (k + 1)]
+
+
+def line_kernel(r_ref, out_ref, mine_ref):
+    zh, zl = lax.axis_index("zh"), lax.axis_index("zl")
+    total = r_ref[0, 0:SHARED]
     for k in range(1, PLANE):
-        total += r_ref[k, 0:CHUNK]
-    rows = jnp.zeros((ROWS_AT, C), F32)
-    cols = jnp.zeros((COLS_AT, C), F32)
-    for j in range(4):
-        rows += jnp.where(j == y, row_ref[...], r_ref[4 * x + j, CHUNK:CHUNK + ROWS_AT])
-        cols += r_ref[4 * j + y, CHUNK:]
+        total += r_ref[k, 0:SHARED]
+    for i in range(4):
+        part = r_ref[i, CHUNK:]
+        for j in range(1, 4):
+            part += r_ref[4 * j + i, CHUNK:]
+        mine_ref[COLS_AT * i:COLS_AT * (i + 1)] = part
     for k in range(LINE):
-        out_ref[k, 0:CHUNK] = total
-        out_ref[k, CHUNK:] = jnp.zeros((COLS_AT, C), F32)
-    out_ref[4 * (1 - zh) + zl, CHUNK:] = cols
-    for j in range(4):
-        out_ref[4 * zh + j, CHUNK:CHUNK + ROWS_AT] = rows
-    mine_ref[...] = cols
-
-
-def spread_kernel(r_ref, col_ref, out_ref, mine_ref):
-    x, y, zh, zl = [lax.axis_index(a) for a in ("x", "y", "zh", "zl")]
-    total = r_ref[0, 0:CHUNK]
+        out_ref[k, 0:SHARED] = total
+        out_ref[k, SHARED:] = jnp.zeros((4 * COLS_AT, C), F32)
+    for i in range(4):
+        part = r_ref[4 * i, SHARED:CHUNK]
+        for j in range(1, 4):
+            part += r_ref[4 * i + j, SHARED:CHUNK]
+        at = SHARED + ROWS_AT * i
+        for j in range(4):
+            out_ref[4 * zh + j, at:at + ROWS_AT] = part
+    out_ref[4 * (1 - zh) + zl, SHARED:] = mine_ref[...]
+
+
+def spread_kernel(r_ref, mine_ref, out_ref):
+    zh, zl = lax.axis_index("zh"), lax.axis_index("zl")
+    total = r_ref[0, 0:SHARED]
     for k in range(1, LINE):
-        total += r_ref[k, 0:CHUNK]
-    rows = r_ref[4 * zh, CHUNK:CHUNK + ROWS_AT]
+        total += r_ref[k, 0:SHARED]
+    rows = r_ref[4 * zh, SHARED:SHARED + 4 * ROWS_AT]
     for j in range(1, 4):
-        rows += r_ref[4 * zh + j, CHUNK:CHUNK + ROWS_AT]
-    cols = col_ref[...] + r_ref[4 * (1 - zh) + zl, CHUNK:]
+        rows += r_ref[4 * zh + j, SHARED:SHARED + 4 * ROWS_AT]
+    cols = mine_ref[...] + r_ref[4 * (1 - zh) + zl, SHARED:]
     for k in range(PLANE):
-        out_ref[k, 0:CHUNK] = total
-        out_ref[k, CHUNK:] = jnp.zeros((COLS_AT, C), F32)
-    for j in range(4):
-        out_ref[4 * j + y, CHUNK:] = cols
-    for j in range(4):
-        out_ref[4 * x + j, CHUNK:CHUNK + ROWS_AT] = rows
-    mine_ref[...] = cols
-
-
-def glue(kernel, name, parts, mine, *args):
+        i, j = k // 4, k % 4
+        out_ref[k, 0:SHARED] = total
+        out_ref[k, SHARED:CHUNK] = rows[ROWS_AT * i:ROWS_AT * (i + 1)]
+        out_ref[k, CHUNK:] = cols[COLS_AT * j:COLS_AT * (j + 1)]
+
+
+def glue(kernel, name, outs, *args):
     vmem = pl.BlockSpec(memory_space=pltpu.VMEM)
     return pl.pallas_call(
         kernel,
         in_specs=[vmem] * len(args),
-        out_specs=[vmem] * 2,
-        out_shape=[jax.ShapeDtypeStruct((parts, WIDE, C), F32), jax.ShapeDtypeStruct((mine, C), F32)],
+        out_specs=[vmem] * len(outs),
+        out_shape=[jax.ShapeDtypeStruct(shape + (C,), F32) for shape in outs],
         compiler_params=pltpu.CompilerParams(vmem_limit_bytes=16 * 1024 * 1024),
         name=name,
     )(*args)
 
 
-def final_kernel(own_ref, other_ref, col_ref, wr_ref, wc_ref, w_ref,
+def final_kernel(own_ref, other_ref, wr_ref, wc_ref, w_ref,
                  dsr_ref, dsc_ref, dwr_ref, dwc_ref, rec_ref, rel_ref, dg_ref, db_ref, buf, m, rows, cols, rel):
-    core, x, y = [lax.axis_index(a) for a in ("c", "x", "y")]
+    core = lax.axis_index("c")
     buf[core] = own_ref[...]
     buf[1 - core] = other_ref[...]
     for k in range(PARTS):
@@ -289,12 +279,9 @@
         lo, hi = 5 * k, min(5 * k + 5, 144)
         if lo < hi:
             rel[lo:hi] = buf[half, place, 28:28 + hi - lo]
-    for half in range(2):
-        for j in range(4):
-            at = ROWS_AT * (4 * half + j)
-            rows[at:at + ROWS_AT] = buf[half, 4 * x + j, CHUNK:CHUNK + ROWS_AT]
-    for j in range(4):
-        cols[COLS_AT * j:COLS_AT * (j + 1)] = jnp.where(j == x, col_ref[...], own_ref[4 * j + y, CHUNK:])
+        rows[ROWS_AT * k:ROWS_AT * (k + 1)] = buf[half, place, SHARED:CHUNK]
+    for k in range(PLANE):
+        cols[COLS_AT * k:COLS_AT * (k + 1)] = own_ref[k, CHUNK:]
     rel_ref[...] = rel[0:BINS]
     total = jnp.sum(rel[133:139], axis=0, keepdims=True)
     w = w_ref[...].astype(F32)
@@ -305,12 +292,12 @@
     dsc_ref[...] = split_dot(cols[...], wc_ref[...], ((1,), (1,)), True)
 
 
-def finish(own, other, col, wr, wc, w, nrows, ncols):
+def finish(own, other, wr, wc, w, nrows, ncols):
     f = lambda *s: jax.ShapeDtypeStruct(s, F32)
     vmem = pl.BlockSpec(memory_space=pltpu.VMEM)
     return pl.pallas_call(
         final_kernel,
-        in_specs=[vmem] * 6,
+        in_specs=[vmem] * 5,
         out_specs=[vmem] * 8,
         out_shape=[f(nrows, S), f(ncols, S), f(S, C), f(S, C), f(C, C), f(BINS, C), f(1, C), f(1, C)],
         scratch_shapes=[
@@ -322,7 +309,7 @@
         ],
         compiler_params=pltpu.CompilerParams(vmem_limit_bytes=16 * 1024 * 1024),
         name="finish",
-    )(own, other, col, wr, wc, w)
+    )(own, other, wr, wc, w)
 
 
 def swap(a):
@@ -335,11 +322,13 @@
     send, keep, col_part, d_prev = local_reductions(
         cot, prev, w_rec, gain2, bias2, ids_rows, ids_cols, single_rows, single_cols
     )
-    shares, row_mine = glue(plane_kernel, "plane", PLANE, ROWS_AT, keep, swap(send), col_part)
-    shares, col_mine = glue(line_kernel, "line", LINE, COLS_AT, lax.all_to_all(shares, XY, 0, 0), row_mine)
-    shares, col_mine = glue(spread_kernel, "spread", PLANE, COLS_AT, lax.all_to_all(shares, Z, 0, 0), col_mine)
+    (shares,) = glue(plane_kernel, "plane", [(PLANE, WIDE)], keep, swap(send), col_part)
+    got = lax.all_to_all(shares, XY, 0, 0)
+    shares, mine = glue(line_kernel, "line", [(LINE, SHARED + 4 * COLS_AT), (4 * COLS_AT,)], got)
+    got = lax.all_to_all(shares, Z, 0, 0)
+    (shares,) = glue(spread_kernel, "spread", [(PLANE, WIDE)], got, mine)
     own = lax.all_to_all(shares, XY, 0, 0)
-    dsr, dsc, dwr, dwc, rec, rel, dg, db = finish(own, swap(own), col_mine, w_row, w_col, w_rec, nrows, ncols)
+    dsr, dsc, dwr, dwc, rec, rel, dg, db = finish(own, swap(own), w_row, w_col, w_rec, nrows, ncols)
     return d_prev, dsr, dsc, dwr, dwc, rec, rel, dg.reshape(C), db.reshape(C)
 
 

time: 68.7 us -> 66.1 us (0.962)
  blocking collectives: 45.1 us -> 42.7 us
    all_to_all x1, blocking collectives: 12.5 us -> 11.3 us  [shards(): own = lax.all_to_all(shares, XY, 0, 0)]
    all_to_all x2, blocking collectives: 32.6 us -> 31.5 us  [the longest x1 17.4 us: shards(): got = lax.all_to_all(shares, Z, 0, 0)]
where the time goes in v5:
time: 66.1 us; the launch traced here: 65.9 us
  blocking collectives  42.7 us (65%)
  Pallas kernels  11.8 us (18%)
  starting transfers between devices  8.12 us (12%)
  waiting for transfers between devices  2.57 us (4%)
  between operations  0.69 us (1%)
    all_to_all x1, blocking collectives, shards(): got = lax.all_to_all(shares, Z, 0, 0)  17.4 us
    all_to_all x1, blocking collectives, shards(): got = lax.all_to_all(shares, XY, 0, 0)  14.1 us
    all_to_all x1, blocking collectives, shards(): own = lax.all_to_all(shares, XY, 0, 0)  11.3 us
    pallas_call x1, Pallas kernels, local_reductions(): pl.pallas_call(functools.partial(reduce_kernel, cols, rows), in_specs=[hb...  10.5 us
    ppermute x2, starting transfers between devices, swap(): return lax.ppermute(a, 'c', [(0, 1), (1, 0)])  8.12 us
    ppermute x2, waiting for transfers between devices, swap(): return lax.ppermute(a, 'c', [(0, 1), (1, 0)])  2.57 us
  transfers between devices with their start and end apart: 2, of which 2 were waited for; matrix products, arithmetic and copies ran while one was open for 0% of the time, Pallas kernels for 0%

profile of v5, /device:TPU:1, one launch (start us, length us, event | category | flops | bytes accessed | tf_op | source)
XLA Modules:
  0.0 65.9 jit_solution(17448336484180643286)
XLA Ops:
  0.6 10.5 %local_reductions.1 = (f32[592,128]{1,0:T(8,128)S(1)}, f32[592,128]{1,0:T(8,128)S(1)}, f32[112,128]{1,0:T(8,128)S(1)}, bf16[128,112,128]{2,1,0:T(8,128)(2,1)}) custom-call(bf16[128,112,128]{2,1,0:T(8,128)(2,1)} %cot_hbm.1, bf16[128,112,128]{2,1,0:T(8,128)(2,1)} %prev_hbm.1, bf16[128,128]{1,0:T(8,128)(2,1)} %w_ref.1, f32[1,128]{1,0:T(1,128)} %bitcast.4, ...), custom_call_target="tpu_custom_call" | custom-call | tf_op jit(solution)/shard_map/local_reductions/pallas_call | solution.py:190
  11.1 0.0 copy-start
  11.2 0.0 copy-start.1
  11.2 0.0 copy-start.2
  11.2 3.3 %collective-permute-start = (f32[592,128]{1,0:T(8,128)S(1)}, f32[592,128]{1,0:T(8,128)S(1)}, u32[]{:S(2)}, u32[]{:S(2)}) collective-permute-start(f32[592,128]{1,0:T(8,128)S(1)} %get-tuple-element.25), channel_id=1, source_target_pairs={{0,1},{1,0},{2,3},{3,2},{4,5},{5,4},{6,7},{7,6},{8,9},{9,8},{10,11... | collective-permute-start | bytes 909320 | tf_op jit(solution)/shard_map/ppermute | solution.py:316
  14.5 1.2 %collective-permute-done.got_ref = f32[592,128]{1,0:T(8,128)S(1)} collective-permute-done((f32[592,128]{1,0:T(8,128)S(1)}, f32[592,128]{1,0:T(8,128)S(1)}, u32[]{:S(2)}, u32[]{:S(2)}) %collective-permute-start) | collective-permute-done | bytes 303136 | tf_op jit(solution)/shard_map/ppermute | solution.py:316
  15.7 0.1 plane.1
  15.8 14.1 %all_to_all.15.r_ref = f32[16,44,128]{2,1,0:T(8,128)S(1)} all-to-all(f32[16,44,128]{2,1,0:T(8,128)S(1)} %plane.1), channel_id=1, replica_groups=mesh['zh'=2,'x'=4,'y'=4,'zl'=4,'c'=2] {'x','y'}, dimensions={0} | all-to-all | bytes 720896 | tf_op jit(solution)/shard_map/all_to_all | solution.py:326
  29.9 17.4 %all_to_all.16.r_ref = f32[8,61,128]{2,1,0:T(8,128)S(1)} all-to-all(f32[8,61,128]{2,1,0:T(8,128)S(1)} %get-tuple-element.27), channel_id=1, replica_groups=mesh['zh'=2,'x'=4,'y'=4,'zl'=4,'c'=2] {'zh','zl'}, dimensions={0} | all-to-all | bytes 499712 | tf_op jit(solution)/shard_map/all_to_all | solution.py:328
  47.4 11.3 %all_to_all.17.own_ref = f32[16,44,128]{2,1,0:T(8,128)S(1)} all-to-all(f32[16,44,128]{2,1,0:T(8,128)S(1)} %spread.1), channel_id=1, replica_groups=mesh['zh'=2,'x'=4,'y'=4,'zl'=4,'c'=2] {'x','y'}, dimensions={0} | all-to-all | bytes 720896 | tf_op jit(solution)/shard_map/all_to_all | solution.py:330
  58.6 4.8 %collective-permute-start.1 = (f32[16,44,128]{2,1,0:T(8,128)S(1)}, f32[16,44,128]{2,1,0:T(8,128)S(1)}, u32[]{:S(2)}, u32[]{:S(2)}) collective-permute-start(f32[16,44,128]{2,1,0:T(8,128)S(1)} %all_to_all.17.own_ref), channel_id=1, source_target_pairs={{0,1},{1,0},{2,3},{3,2},{4,5},{5,4},{6,7},{7,6},{8,9},{9,8},{10,11... | collective-permute-start | bytes 1081352 | tf_op jit(solution)/shard_map/ppermute | solution.py:316
  63.4 1.3 %collective-permute-done.1.other_ref = f32[16,44,128]{2,1,0:T(8,128)S(1)} collective-permute-done((f32[16,44,128]{2,1,0:T(8,128)S(1)}, f32[16,44,128]{2,1,0:T(8,128)S(1)}, u32[]{:S(2)}, u32[]{:S(2)}) %collective-permute-start.1) | collective-permute-done | bytes 360480 | tf_op jit(solution)/shard_map/ppermute | solution.py:316
  64.8 0.0 copy-done
  64.8 0.0 copy-done.1
  64.8 0.0 copy-done.2
  64.8 1.2 %finish.1 = (f32[128,384]{1,0:T(8,128)}, f32[112,384]{1,0:T(8,128)}, f32[384,128]{1,0:T(8,128)}, f32[384,128]{1,0:T(8,128)}, f32[128,128]{1,0:T(8,128)}, /*index...) custom-call(f32[16,44,128]{2,1,0:T(8,128)S(1)} %all_to_all.17.own_ref, ...), custom_call_target="tpu_custom_call" | custom-call | tf_op jit(solution)/shard_map/finish/pallas_call | solution.py:298
  (2 shorter events, 0.1 us)
Async XLA Ops:
  11.1 53.6 %copy-start = (bf16[128,128]{1,0:T(8,128)(2,1)S(1)}, bf16[128,128]{1,0:T(8,128)(2,1)}, u32[]{:S(2)}) copy-start(bf16[128,128]{1,0:T(8,128)(2,1)} %w_ref.1) | copy-start | bytes 98308
  11.2 53.6 %copy-start.1 = (bf16[384,128]{1,0:T(8,128)(2,1)S(1)}, bf16[384,128]{1,0:T(8,128)(2,1)}, u32[]{:S(2)}) copy-start(bf16[384,128]{1,0:T(8,128)(2,1)} %wr_ref.1) | copy-start | bytes 294916
  11.2 53.6 %copy-start.2 = (bf16[384,128]{1,0:T(8,128)(2,1)S(1)}, bf16[384,128]{1,0:T(8,128)(2,1)}, u32[]{:S(2)}) copy-start(bf16[384,128]{1,0:T(8,128)(2,1)} %wc_ref.1) | copy-start | bytes 294916
  11.2 4.6 %collective-permute-start = (f32[592,128]{1,0:T(8,128)S(1)}, f32[592,128]{1,0:T(8,128)S(1)}, u32[]{:S(2)}, u32[]{:S(2)}) collective-permute-start(f32[592,128]{1,0:T(8,128)S(1)} %get-tuple-element.25), channel_id=1, source_target_pairs={{0,1},{1,0},{2,3},{3,2},{4,5},{5,4},{6,7},{7,6},{8,9},{9,8},{10,11... | collective-permute-start | bytes 909320 | tf_op jit(solution)/shard_map/ppermute | solution.py:316
  58.6 6.1 %collective-permute-start.1 = (f32[16,44,128]{2,1,0:T(8,128)S(1)}, f32[16,44,128]{2,1,0:T(8,128)S(1)}, u32[]{:S(2)}, u32[]{:S(2)}) collective-permute-start(f32[16,44,128]{2,1,0:T(8,128)S(1)} %all_to_all.17.own_ref), channel_id=1, source_target_pairs={{0,1},{1,0},{2,3},{3,2},{4,5},{5,4},{6,7},{7,6},{8,9},{9,8},{10,11... | collective-permute-start | bytes 1081352 | tf_op jit(solution)/shard_map/ppermute | solution.py:316

commit v6 on v5

--- a/solution.py
+++ b/solution.py
@@ -94,16 +94,7 @@
     def mean(a):
         return jnp.sum(a, axis=0, keepdims=True) * (1.0 / C)
 
-    @pl.loop(0, units, unroll=8)
-    def _(u):
-        for copy in fetch(u):
-            copy.wait()
-
-        @pl.when(u + 2 < units)
-        def _():
-            for copy in fetch(u + 2):
-                copy.start()
-
+    def unit(u):
         first = u * SUB
         here = part(u)
         cot = cot_ref[here].reshape(n, C)
@@ -121,7 +112,6 @@
         gains[...] += share
         res = (rstd * (g - g_mean - xhat * mean(gx))).astype(BF16)
         dprev_ref[here] = jnp.transpose(res).reshape(SUB, cols, C)
-        put(u).start()
         mask = lane == sub + first
         di = [jnp.sum(jnp.where(mask, idr[k:k + 1], 0.0), axis=1, keepdims=True) for k in range(5)]
         dj = [idc[k:k + 1] for k in range(5)]
@@ -137,11 +127,12 @@
         e = jnp.where(packed >= 1 << 18, 132, -1)
 
         def hot(lo, hi, *codes):
-            q = lax.broadcasted_iota(jnp.int32, (hi - lo, n), 0) + lo
+            q = (lax.broadcasted_iota(jnp.int32, (hi - lo, n), 0) + lo).astype(BF16)
+            codes = [code.astype(BF16) for code in codes]
             hit = q == codes[0]
             for code in codes[1:]:
                 hit = hit | (q == code)
-            return jnp.where(hit, 1.0, 0.0).astype(BF16)
+            return jnp.where(hit, jnp.ones((), BF16), jnp.zeros((), BF16))
 
         left = jnp.concatenate(
             [normed, hot(0, 64, r), hot(64, 80, r, t), hot(80, 128, t), hot(128, 144, t, e, c), rowind], axis=0
@@ -153,6 +144,23 @@
         for s in range(1, SUB):
             wide += cot[s * cols:(s + 1) * cols].astype(F32)
         colp_ref[...] += wide
+
+    @pl.loop(0, units // 2, unroll=1)
+    def _(v):
+        for j in range(2):
+            for copy in fetch(v * 2 + j):
+                copy.wait()
+
+        @pl.when(v + 1 < units // 2)
+        def _():
+            for j in range(2):
+                for copy in fetch((v + 1) * 2 + j):
+                    copy.start()
+
+        for j in range(2):
+            unit(v * 2 + j)
+        for j in range(2):
+            put(v * 2 + j).start()
 
     for copy in small[5:]:
         copy.wait()

time: 66.1 us -> 65.7 us (level)
  no operation moved by 1% of the time
where the time goes in v6:
time: 65.7 us; the launch traced here: 65.4 us
  blocking collectives  42.7 us (65%)
  Pallas kernels  11.3 us (17%)
  starting transfers between devices  8.12 us (12%)
  waiting for transfers between devices  2.57 us (4%)
  between operations  0.69 us (1%)
    all_to_all x1, blocking collectives, shards(): got = lax.all_to_all(shares, Z, 0, 0)  17.4 us
    all_to_all x1, blocking collectives, shards(): got = lax.all_to_all(shares, XY, 0, 0)  14.1 us
    all_to_all x1, blocking collectives, shards(): own = lax.all_to_all(shares, XY, 0, 0)  11.3 us
    pallas_call x1, Pallas kernels, local_reductions(): pl.pallas_call(functools.partial(reduce_kernel, cols, rows), in_specs=[hb...  10 us
    ppermute x2, starting transfers between devices, swap(): return lax.ppermute(a, 'c', [(0, 1), (1, 0)])  8.12 us
    ppermute x2, waiting for transfers between devices, swap(): return lax.ppermute(a, 'c', [(0, 1), (1, 0)])  2.57 us
  transfers between devices with their start and end apart: 2, of which 2 were waited for; matrix products, arithmetic and copies ran while one was open for 0% of the time, Pallas kernels for 0%

profile of v6, /device:TPU:1, one launch (start us, length us, event | category | flops | bytes accessed | tf_op | source)
XLA Modules:
  0.0 65.4 jit_solution(16382394531583208629)
XLA Ops:
  0.6 10.0 %local_reductions.1 = (f32[592,128]{1,0:T(8,128)S(1)}, f32[592,128]{1,0:T(8,128)S(1)}, f32[112,128]{1,0:T(8,128)S(1)}, bf16[128,112,128]{2,1,0:T(8,128)(2,1)}) custom-call(bf16[128,112,128]{2,1,0:T(8,128)(2,1)} %cot_hbm.1, bf16[128,112,128]{2,1,0:T(8,128)(2,1)} %prev_hbm.1, bf16[128,128]{1,0:T(8,128)(2,1)} %w_ref.1, f32[1,128]{1,0:T(1,128)} %bitcast.4, ...), custom_call_target="tpu_custom_call" | custom-call | tf_op jit(solution)/shard_map/local_reductions/pallas_call | solution.py:198
  10.7 0.0 copy-start
  10.7 0.0 copy-start.1
  10.7 0.0 copy-start.2
  10.7 3.3 %collective-permute-start = (f32[592,128]{1,0:T(8,128)S(1)}, f32[592,128]{1,0:T(8,128)S(1)}, u32[]{:S(2)}, u32[]{:S(2)}) collective-permute-start(f32[592,128]{1,0:T(8,128)S(1)} %get-tuple-element.25), channel_id=1, source_target_pairs={{0,1},{1,0},{2,3},{3,2},{4,5},{5,4},{6,7},{7,6},{8,9},{9,8},{10,11... | collective-permute-start | bytes 909320 | tf_op jit(solution)/shard_map/ppermute | solution.py:324
  14.0 1.2 %collective-permute-done.got_ref = f32[592,128]{1,0:T(8,128)S(1)} collective-permute-done((f32[592,128]{1,0:T(8,128)S(1)}, f32[592,128]{1,0:T(8,128)S(1)}, u32[]{:S(2)}, u32[]{:S(2)}) %collective-permute-start) | collective-permute-done | bytes 303136 | tf_op jit(solution)/shard_map/ppermute | solution.py:324
  15.2 0.1 plane.1
  15.3 14.1 %all_to_all.15.r_ref = f32[16,44,128]{2,1,0:T(8,128)S(1)} all-to-all(f32[16,44,128]{2,1,0:T(8,128)S(1)} %plane.1), channel_id=1, replica_groups=mesh['zh'=2,'x'=4,'y'=4,'zl'=4,'c'=2] {'x','y'}, dimensions={0} | all-to-all | bytes 720896 | tf_op jit(solution)/shard_map/all_to_all | solution.py:334
  29.4 17.4 %all_to_all.16.r_ref = f32[8,61,128]{2,1,0:T(8,128)S(1)} all-to-all(f32[8,61,128]{2,1,0:T(8,128)S(1)} %get-tuple-element.27), channel_id=1, replica_groups=mesh['zh'=2,'x'=4,'y'=4,'zl'=4,'c'=2] {'zh','zl'}, dimensions={0} | all-to-all | bytes 499712 | tf_op jit(solution)/shard_map/all_to_all | solution.py:336
  46.9 11.3 %all_to_all.17.own_ref = f32[16,44,128]{2,1,0:T(8,128)S(1)} all-to-all(f32[16,44,128]{2,1,0:T(8,128)S(1)} %spread.1), channel_id=1, replica_groups=mesh['zh'=2,'x'=4,'y'=4,'zl'=4,'c'=2] {'x','y'}, dimensions={0} | all-to-all | bytes 720896 | tf_op jit(solution)/shard_map/all_to_all | solution.py:338
  58.1 4.8 %collective-permute-start.1 = (f32[16,44,128]{2,1,0:T(8,128)S(1)}, f32[16,44,128]{2,1,0:T(8,128)S(1)}, u32[]{:S(2)}, u32[]{:S(2)}) collective-permute-start(f32[16,44,128]{2,1,0:T(8,128)S(1)} %all_to_all.17.own_ref), channel_id=1, source_target_pairs={{0,1},{1,0},{2,3},{3,2},{4,5},{5,4},{6,7},{7,6},{8,9},{9,8},{10,11... | collective-permute-start | bytes 1081352 | tf_op jit(solution)/shard_map/ppermute | solution.py:324
  62.9 1.3 %collective-permute-done.1.other_ref = f32[16,44,128]{2,1,0:T(8,128)S(1)} collective-permute-done((f32[16,44,128]{2,1,0:T(8,128)S(1)}, f32[16,44,128]{2,1,0:T(8,128)S(1)}, u32[]{:S(2)}, u32[]{:S(2)}) %collective-permute-start.1) | collective-permute-done | bytes 360480 | tf_op jit(solution)/shard_map/ppermute | solution.py:324
  64.3 0.0 copy-done
  64.3 0.0 copy-done.1
  64.3 0.0 copy-done.2
  64.3 1.2 %finish.1 = (f32[128,384]{1,0:T(8,128)}, f32[112,384]{1,0:T(8,128)}, f32[384,128]{1,0:T(8,128)}, f32[384,128]{1,0:T(8,128)}, f32[128,128]{1,0:T(8,128)}, /*index...) custom-call(f32[16,44,128]{2,1,0:T(8,128)S(1)} %all_to_all.17.own_ref, ...), custom_call_target="tpu_custom_call" | custom-call | tf_op jit(solution)/shard_map/finish/pallas_call | solution.py:306
  (2 shorter events, 0.1 us)
Async XLA Ops:
  10.7 53.6 %copy-start = (bf16[128,128]{1,0:T(8,128)(2,1)S(1)}, bf16[128,128]{1,0:T(8,128)(2,1)}, u32[]{:S(2)}) copy-start(bf16[128,128]{1,0:T(8,128)(2,1)} %w_ref.1) | copy-start | bytes 98308
  10.7 53.6 %copy-start.1 = (bf16[384,128]{1,0:T(8,128)(2,1)S(1)}, bf16[384,128]{1,0:T(8,128)(2,1)}, u32[]{:S(2)}) copy-start(bf16[384,128]{1,0:T(8,128)(2,1)} %wr_ref.1) | copy-start | bytes 294916
  10.7 53.6 %copy-start.2 = (bf16[384,128]{1,0:T(8,128)(2,1)S(1)}, bf16[384,128]{1,0:T(8,128)(2,1)}, u32[]{:S(2)}) copy-start(bf16[384,128]{1,0:T(8,128)(2,1)} %wc_ref.1) | copy-start | bytes 294916
  10.7 4.5 %collective-permute-start = (f32[592,128]{1,0:T(8,128)S(1)}, f32[592,128]{1,0:T(8,128)S(1)}, u32[]{:S(2)}, u32[]{:S(2)}) collective-permute-start(f32[592,128]{1,0:T(8,128)S(1)} %get-tuple-element.25), channel_id=1, source_target_pairs={{0,1},{1,0},{2,3},{3,2},{4,5},{5,4},{6,7},{7,6},{8,9},{9,8},{10,11... | collective-permute-start | bytes 909320 | tf_op jit(solution)/shard_map/ppermute | solution.py:324
  58.1 6.1 %collective-permute-start.1 = (f32[16,44,128]{2,1,0:T(8,128)S(1)}, f32[16,44,128]{2,1,0:T(8,128)S(1)}, u32[]{:S(2)}, u32[]{:S(2)}) collective-permute-start(f32[16,44,128]{2,1,0:T(8,128)S(1)} %all_to_all.17.own_ref), channel_id=1, source_target_pairs={{0,1},{1,0},{2,3},{3,2},{4,5},{5,4},{6,7},{7,6},{8,9},{9,8},{10,11... | collective-permute-start | bytes 1081352 | tf_op jit(solution)/shard_map/ppermute | solution.py:324

commit v7 on v6

--- a/solution.py
+++ b/solution.py
@@ -19,7 +19,7 @@
 PARTS = 32
 PLANE, LINE = 16, 8
 VMEM = 40 * 1024 * 1024
-XY, Z = ("x", "y"), ("zh", "zl")
+XY, Z = ("x", "y"), ("zl", "zh")
 ROW, COL = ("zh", "x"), ("y", "zl", "c")
 
 
@@ -242,8 +242,8 @@
             part += r_ref[4 * i + j, SHARED:CHUNK]
         at = SHARED + ROWS_AT * i
         for j in range(4):
-            out_ref[4 * zh + j, at:at + ROWS_AT] = part
-    out_ref[4 * (1 - zh) + zl, SHARED:] = mine_ref[...]
+            out_ref[2 * j + zh, at:at + ROWS_AT] = part
+    out_ref[2 * zl + 1 - zh, SHARED:] = mine_ref[...]
 
 
 def spread_kernel(r_ref, mine_ref, out_ref):
@@ -251,10 +251,10 @@
     total = r_ref[0, 0:SHARED]
     for k in range(1, LINE):
         total += r_ref[k, 0:SHARED]
-    rows = r_ref[4 * zh, SHARED:SHARED + 4 * ROWS_AT]
+    rows = r_ref[zh, SHARED:SHARED + 4 * ROWS_AT]
     for j in range(1, 4):
-        rows += r_ref[4 * zh + j, SHARED:SHARED + 4 * ROWS_AT]
-    cols = mine_ref[...] + r_ref[4 * (1 - zh) + zl, SHARED:]
+        rows += r_ref[2 * j + zh, SHARED:SHARED + 4 * ROWS_AT]
+    cols = mine_ref[...] + r_ref[2 * zl + 1 - zh, SHARED:]
     for k in range(PLANE):
         i, j = k // 4, k % 4
         out_ref[k, 0:SHARED] = total
@@ -274,8 +274,27 @@
     )(*args)
 
 
-def final_kernel(own_ref, other_ref, wr_ref, wc_ref, w_ref,
-                 dsr_ref, dsc_ref, dwr_ref, dwc_ref, rec_ref, rel_ref, dg_ref, db_ref, buf, m, rows, cols, rel):
+def cols_kernel(own_ref, wc_ref, dsc_ref, cols):
+    for k in range(PLANE):
+        cols[COLS_AT * k:COLS_AT * (k + 1)] = own_ref[k, CHUNK:]
+    dsc_ref[...] = split_dot(cols[...], wc_ref[...], ((1,), (1,)), True)
+
+
+def finish_cols(own, wc, ncols):
+    vmem = pl.BlockSpec(memory_space=pltpu.VMEM)
+    return pl.pallas_call(
+        cols_kernel,
+        in_specs=[vmem] * 2,
+        out_specs=vmem,
+        out_shape=jax.ShapeDtypeStruct((ncols, S), F32),
+        scratch_shapes=[pltpu.VMEM((ncols, C), F32)],
+        compiler_params=pltpu.CompilerParams(vmem_limit_bytes=16 * 1024 * 1024),
+        name="finish_cols",
+    )(own, wc)
+
+
+def final_kernel(own_ref, other_ref, wr_ref, w_ref,
+                 dsr_ref, dwr_ref, dwc_ref, rec_ref, rel_ref, dg_ref, db_ref, buf, m, rows, rel):
     core = lax.axis_index("c")
     buf[core] = own_ref[...]
     buf[1 - core] = other_ref[...]
@@ -288,8 +307,6 @@
         if lo < hi:
             rel[lo:hi] = buf[half, place, 28:28 + hi - lo]
         rows[ROWS_AT * k:ROWS_AT * (k + 1)] = buf[half, place, SHARED:CHUNK]
-    for k in range(PLANE):
-        cols[COLS_AT * k:COLS_AT * (k + 1)] = own_ref[k, CHUNK:]
     rel_ref[...] = rel[0:BINS]
     total = jnp.sum(rel[133:139], axis=0, keepdims=True)
     w = w_ref[...].astype(F32)
@@ -297,27 +314,25 @@
     dg_ref[...] = rel[BINS:BINS + 1]
     db_ref[...] = jnp.sum(jnp.transpose(w * total), axis=0, keepdims=True)
     dsr_ref[...] = split_dot(rows[...], wr_ref[...], ((1,), (1,)), True)
-    dsc_ref[...] = split_dot(cols[...], wc_ref[...], ((1,), (1,)), True)
-
-
-def finish(own, other, wr, wc, w, nrows, ncols):
+
+
+def finish(own, other, wr, w, nrows):
     f = lambda *s: jax.ShapeDtypeStruct(s, F32)
     vmem = pl.BlockSpec(memory_space=pltpu.VMEM)
     return pl.pallas_call(
         final_kernel,
-        in_specs=[vmem] * 5,
-        out_specs=[vmem] * 8,
-        out_shape=[f(nrows, S), f(ncols, S), f(S, C), f(S, C), f(C, C), f(BINS, C), f(1, C), f(1, C)],
+        in_specs=[vmem] * 4,
+        out_specs=[vmem] * 7,
+        out_shape=[f(nrows, S), f(S, C), f(S, C), f(C, C), f(BINS, C), f(1, C), f(1, C)],
         scratch_shapes=[
             pltpu.VMEM((2, PLANE, WIDE, C), F32),
             pltpu.VMEM((C, C), F32),
             pltpu.VMEM((nrows, C), F32),
-            pltpu.VMEM((ncols, C), F32),
             pltpu.VMEM((144, C), F32),
         ],
         compiler_params=pltpu.CompilerParams(vmem_limit_bytes=16 * 1024 * 1024),
         name="finish",
-    )(own, other, wr, wc, w)
+    )(own, other, wr, w)
 
 
 def swap(a):
@@ -336,7 +351,8 @@
     got = lax.all_to_all(shares, Z, 0, 0)
     (shares,) = glue(spread_kernel, "spread", [(PLANE, WIDE)], got, mine)
     own = lax.all_to_all(shares, XY, 0, 0)
-    dsr, dsc, dwr, dwc, rec, rel, dg, db = finish(own, swap(own), w_row, w_col, w_rec, nrows, ncols)
+    dsc = finish_cols(own, w_col, ncols)
+    dsr, dwr, dwc, rec, rel, dg, db = finish(own, swap(own), w_row, w_rec, nrows)
     return d_prev, dsr, dsc, dwr, dwc, rec, rel, dg.reshape(C), db.reshape(C)
 
 

time: 65.7 us -> 63.1 us (0.960)
  blocking collectives: 42.7 us -> 40.4 us
  waiting for transfers between devices: 2.57 us -> 1.68 us
  Pallas kernels: 11.3 us -> 12.1 us
    all_to_all x1, blocking collectives: 17.4 us -> 15.1 us  [shards(): got = lax.all_to_all(shares, Z, 0, 0)]
    ppermute x2, waiting for transfers between devices: 2.57 us -> 1.68 us  [swap(): return lax.ppermute(a, 'c', [(0, 1), (1, 0)])]
    pallas_call x1 -> x2, Pallas kernels: 1.16 us -> 1.95 us  [the longest x1 1.06 us: finish(): pl.pallas_call(final_kernel, in_specs=[vmem] * 4, out_specs=[vmem] * 7, o...]
  transfers between devices with their start and end apart: 2 -> 2, of which waited for: 2 -> 2; matrix products, arithmetic and copies ran while one was open for 0% -> 0% of each run, Pallas kernels for 0% -> 1%
where the time goes in v7:
time: 63.1 us; the launch traced here: 62.7 us
  blocking collectives  40.4 us (64%)
  Pallas kernels  12.1 us (19%)
  starting transfers between devices  7.76 us (12%)
  waiting for transfers between devices  1.68 us (3%)
  between operations  0.69 us (1%)
    all_to_all x1, blocking collectives, shards(): got = lax.all_to_all(shares, Z, 0, 0)  15.1 us
    all_to_all x1, blocking collectives, shards(): got = lax.all_to_all(shares, XY, 0, 0)  14.1 us
    all_to_all x1, blocking collectives, shards(): own = lax.all_to_all(shares, XY, 0, 0)  11.3 us
    pallas_call x1, Pallas kernels, local_reductions(): pl.pallas_call(functools.partial(reduce_kernel, cols, rows), in_specs=[hb...  10 us
    ppermute x2, starting transfers between devices, swap(): return lax.ppermute(a, 'c', [(0, 1), (1, 0)])  7.76 us
    ppermute x2, waiting for transfers between devices, swap(): return lax.ppermute(a, 'c', [(0, 1), (1, 0)])  1.68 us
  transfers between devices with their start and end apart: 2, of which 2 were waited for; matrix products, arithmetic and copies ran while one was open for 0% of the time, Pallas kernels for 1%

profile of v7, /device:TPU:1, one launch (start us, length us, event | category | flops | bytes accessed | tf_op | source)
XLA Modules:
  0.0 62.7 jit_solution(7556790982135619447)
XLA Ops:
  0.6 10.0 %local_reductions.1 = (f32[592,128]{1,0:T(8,128)S(1)}, f32[592,128]{1,0:T(8,128)S(1)}, f32[112,128]{1,0:T(8,128)S(1)}, bf16[128,112,128]{2,1,0:T(8,128)(2,1)}) custom-call(bf16[128,112,128]{2,1,0:T(8,128)(2,1)} %cot_hbm.1, bf16[128,112,128]{2,1,0:T(8,128)(2,1)} %prev_hbm.1, bf16[128,128]{1,0:T(8,128)(2,1)} %w_ref.1, f32[1,128]{1,0:T(1,128)} %bitcast.4, ...), custom_call_target="tpu_custom_call" | custom-call | tf_op jit(solution)/shard_map/local_reductions/pallas_call | solution.py:198
  10.7 0.0 copy-start.2
  10.7 0.0 copy-start
  10.7 0.0 copy-start.1
  10.7 3.3 %collective-permute-start = (f32[592,128]{1,0:T(8,128)S(1)}, f32[592,128]{1,0:T(8,128)S(1)}, u32[]{:S(2)}, u32[]{:S(2)}) collective-permute-start(f32[592,128]{1,0:T(8,128)S(1)} %get-tuple-element.24), channel_id=1, source_target_pairs={{0,1},{1,0},{2,3},{3,2},{4,5},{5,4},{6,7},{7,6},{8,9},{9,8},{10,11... | collective-permute-start | bytes 909320 | tf_op jit(solution)/shard_map/ppermute | solution.py:339
  14.0 1.2 %collective-permute-done.got_ref = f32[592,128]{1,0:T(8,128)S(1)} collective-permute-done((f32[592,128]{1,0:T(8,128)S(1)}, f32[592,128]{1,0:T(8,128)S(1)}, u32[]{:S(2)}, u32[]{:S(2)}) %collective-permute-start) | collective-permute-done | bytes 303136 | tf_op jit(solution)/shard_map/ppermute | solution.py:339
  15.2 0.1 plane.1
  15.3 14.1 %all_to_all.15.r_ref = f32[16,44,128]{2,1,0:T(8,128)S(1)} all-to-all(f32[16,44,128]{2,1,0:T(8,128)S(1)} %plane.1), channel_id=1, replica_groups=mesh['zh'=2,'x'=4,'y'=4,'zl'=4,'c'=2] {'x','y'}, dimensions={0} | all-to-all | bytes 720896 | tf_op jit(solution)/shard_map/all_to_all | solution.py:349
  29.4 15.1 %all_to_all.16.r_ref = f32[8,61,128]{2,1,0:T(8,128)S(1)} all-to-all(f32[8,61,128]{2,1,0:T(8,128)S(1)} %get-tuple-element.26), channel_id=1, replica_groups=mesh['zh'=2,'x'=4,'y'=4,'zl'=4,'c'=2] {'zl','zh'}, dimensions={0} | all-to-all | bytes 499712 | tf_op jit(solution)/shard_map/all_to_all | solution.py:351
  44.6 11.3 %all_to_all.17.own_ref = f32[16,44,128]{2,1,0:T(8,128)S(1)} all-to-all(f32[16,44,128]{2,1,0:T(8,128)S(1)} %spread.1), channel_id=1, replica_groups=mesh['zh'=2,'x'=4,'y'=4,'zl'=4,'c'=2] {'x','y'}, dimensions={0} | all-to-all | bytes 720896 | tf_op jit(solution)/shard_map/all_to_all | solution.py:353
  55.8 4.4 %collective-permute-start.1 = (f32[16,44,128]{2,1,0:T(8,128)S(1)}, f32[16,44,128]{2,1,0:T(8,128)S(1)}, u32[]{:S(2)}, u32[]{:S(2)}) collective-permute-start(f32[16,44,128]{2,1,0:T(8,128)S(1)} %all_to_all.17.own_ref), channel_id=1, source_target_pairs={{0,1},{1,0},{2,3},{3,2},{4,5},{5,4},{6,7},{7,6},{8,9},{9,8},{10,11... | collective-permute-start | bytes 1081352 | tf_op jit(solution)/shard_map/ppermute | solution.py:339
  60.3 0.0 copy-done.2
  60.3 0.9 %finish_cols.1 = f32[112,384]{1,0:T(8,128)} custom-call(f32[16,44,128]{2,1,0:T(8,128)S(1)} %all_to_all.17.own_ref, bf16[384,128]{1,0:T(8,128)(2,1)S(1)} %copy-done.2), custom_call_target="tpu_custom_call" | custom-call | tf_op jit(solution)/shard_map/finish_cols/pallas_call | solution.py:285
  61.2 0.5 collective-permute-done.1.other_ref
  61.6 0.0 copy-done
  61.6 0.0 copy-done.1
  61.6 1.1 %finish.1 = (f32[128,384]{1,0:T(8,128)}, f32[384,128]{1,0:T(8,128)}, f32[384,128]{1,0:T(8,128)}, f32[128,128]{1,0:T(8,128)}, f32[139,128]{1,0:T(8,128)}, /*index=5*/f32[1,128]{1,0:T(1,128)}, f32[1,128]{1,0:T(1,128)}) custom-call(f32[16,44,128]{2,1,0:T(8,128)S(1)} %all_to_all.17.own_ref, f32[16,44,128]{2,1,0:T(8,128)S(1)} %collective-permute-done.1.other_ref, ...), custom_call_target="tpu_custom_call" | custom-call | tf_op jit(solution)/shard_map/finish/pallas_call | solution.py:322
  (2 shorter events, 0.1 us)
Async XLA Ops:
  10.7 49.6 %copy-start.2 = (bf16[384,128]{1,0:T(8,128)(2,1)S(1)}, bf16[384,128]{1,0:T(8,128)(2,1)}, u32[]{:S(2)}) copy-start(bf16[384,128]{1,0:T(8,128)(2,1)} %wc_ref.1) | copy-start | bytes 294916
  10.7 50.9 %copy-start = (bf16[128,128]{1,0:T(8,128)(2,1)S(1)}, bf16[128,128]{1,0:T(8,128)(2,1)}, u32[]{:S(2)}) copy-start(bf16[128,128]{1,0:T(8,128)(2,1)} %w_ref.1) | copy-start | bytes 98308
  10.7 50.9 %copy-start.1 = (bf16[384,128]{1,0:T(8,128)(2,1)S(1)}, bf16[384,128]{1,0:T(8,128)(2,1)}, u32[]{:S(2)}) copy-start(bf16[384,128]{1,0:T(8,128)(2,1)} %wr_ref.1) | copy-start | bytes 294916
  10.7 4.5 %collective-permute-start = (f32[592,128]{1,0:T(8,128)S(1)}, f32[592,128]{1,0:T(8,128)S(1)}, u32[]{:S(2)}, u32[]{:S(2)}) collective-permute-start(f32[592,128]{1,0:T(8,128)S(1)} %get-tuple-element.24), channel_id=1, source_target_pairs={{0,1},{1,0},{2,3},{3,2},{4,5},{5,4},{6,7},{7,6},{8,9},{9,8},{10,11... | collective-permute-start | bytes 909320 | tf_op jit(solution)/shard_map/ppermute | solution.py:339
  55.8 5.8 %collective-permute-start.1 = (f32[16,44,128]{2,1,0:T(8,128)S(1)}, f32[16,44,128]{2,1,0:T(8,128)S(1)}, u32[]{:S(2)}, u32[]{:S(2)}) collective-permute-start(f32[16,44,128]{2,1,0:T(8,128)S(1)} %all_to_all.17.own_ref), channel_id=1, source_target_pairs={{0,1},{1,0},{2,3},{3,2},{4,5},{5,4},{6,7},{7,6},{8,9},{9,8},{10,11... | collective-permute-start | bytes 1081352 | tf_op jit(solution)/shard_map/ppermute | solution.py:339
